TPU v7x, 512 devices: a whole 4x4x16 slice. The times are simulated.
512 devices in a mesh: attn: 32 (over x, z_lo, core), ffn: 4 (over z_hi), grp: 4 (over y).
Axes of the slice: x: 4, y: 4, z: 16 (z_hi: 4, z_lo: 4; z = z_hi * 4 + z_lo), core: 2. Of those that a mesh axis runs over, the one named last changes fastest.
Arguments:
- layer_in: bfloat16 [64, 8192], P(None, 'attn'), may hold values from -0.59765625 to 0.59765625
- gain_attn: float32 [8192], P('attn'), may hold values from 0.1 to 1.9
- gain_ffn: float32 [8192], P('attn'), may hold values from 0.1 to 1.9
- w_query: bfloat16 [8192, 8192], P('attn', ('ffn', 'grp')), may hold values from -0.0625 to 0.0625
- w_keyval: bfloat16 [8192, 4, 256], P('attn', 'ffn'), may hold values from -4 to 4
- w_out: bfloat16 [8192, 8192], P(('ffn', 'grp'), 'attn'), may hold values from -0.0625 to 0.0625
- w_gate_up: bfloat16 [8192, 2, 26624], P('attn', None, ('ffn', 'grp')), may hold values from -0.0625 to 0.0625
- w_down: bfloat16 [26624, 8192], P(('ffn', 'grp'), 'attn'), may hold values from -0.0390625 to 0.0390625
- cache: bfloat16 [64, 4, 4096, 256], P('attn', 'ffn', 'grp'), may hold values from -200 to 200
- cache_len: int32 [64], replicated, may hold values from 512 to 4096, as said below
- request_slot: int32 [64], replicated, may hold values from 0 to 63, each once
Outputs:
- layer_out: bfloat16 [64, 8192], P(None, 'attn')
Inputs may be any that keep to these rules, and one draw needn't show every extreme that they name: `cache_len`: at least 512; some request holds exactly 4096.
All inputs are finite; a program needn't handle non-finite values.
Results may differ from a plain program's by a relative error of at most 0.022.
The roundings to bfloat16 on the way count: a program that leaves them out, or rounds other values in their place, can miss the bound.
Values may be sent and summed in bfloat16 or wider, within the bound.
No kernel may reach another device: no remote copies, remote signals or barrier semaphores. Data moves between devices by JAX's collectives and lax.ppermute only.
A program may use at most 64 MiB of HBM per device.

v0:
```python
import jax
import jax.numpy as jnp
from jax import lax
from jax.sharding import PartitionSpec as P

D = 8192


def joined(part, axis, combine):
    gathered = jax.tree.map(lambda a: lax.all_gather(a, axis), part)

    def take(source):
        return jax.tree.map(lambda a: lax.dynamic_index_in_dim(a, source, 0, False), gathered)

    return lax.fori_loop(
        1, lax.axis_size(axis), lambda source, state: combine(state, take(source)), take(0)
    )


def rotate(values, position):
    half = values.shape[-1] // 2
    freqs = 500000.0 ** (-(jnp.arange(half, dtype=jnp.float32) * 2.0 / values.shape[-1]))
    angles = position[:, None] * freqs[None, :]
    cosine = jnp.cos(angles)[:, None, :]
    sine = jnp.sin(angles)[:, None, :]
    first = values[..., :half]
    second = values[..., half:]
    return jnp.concatenate([first * cosine - second * sine, second * cosine + first * sine], -1)


def combine_parts(first, second):
    top = jnp.maximum(first[0], second[0])
    scale_one = jnp.exp(first[0] - top)
    scale_two = jnp.exp(second[0] - top)
    total = first[1] * scale_one + second[1] * scale_two
    mixed = first[2] * scale_one[..., None] + second[2] * scale_two[..., None]
    return (top, total, mixed)


def finish_heads(top, total, mixed, query_mine, key_mine, value_mine, scale):
    own = jnp.sum(query_mine.astype(jnp.float32) * key_mine.astype(jnp.float32), -1) * scale
    best = jnp.maximum(top, own)
    old_scale = jnp.exp(top - best)
    own_weight = jnp.exp(own - best)
    denom = total * old_scale + own_weight
    result = mixed * old_scale[..., None] + own_weight[..., None] * value_mine.astype(jnp.float32)
    return result / denom[..., None]


def shards(
    layer_in,
    gain_attn,
    gain_ffn,
    w_query,
    w_keyval,
    w_out,
    w_gate_up,
    w_down,
    cache,
    cache_len,
    request_slot,
):
    req_total = layer_in.shape[0]
    req_here = cache.shape[0]
    kv_here = cache.shape[1]
    slots_here = cache.shape[2]
    head_size = cache.shape[3] // 2
    query_cols = w_query.shape[1]
    grp_count = lax.axis_size("grp")
    resid = layer_in.astype(jnp.float32)
    squares = lax.psum(jnp.sum(resid * resid, axis=1), "attn")
    normed = (resid * lax.rsqrt(squares / D + 1e-05)[:, None] * gain_attn).astype(jnp.bfloat16)
    order = jnp.arange(req_total, dtype=jnp.int32)
    matches = request_slot[None, :] == order[:, None]
    slot_owner = jnp.sum(jnp.where(matches, order[None, :], 0), axis=1)
    slot_length = jnp.sum(jnp.where(matches, cache_len[None, :], 0), axis=1)
    slot_rows = jnp.take(normed, slot_owner, axis=0)
    keyval_flat = w_keyval.reshape(w_keyval.shape[0], -1)
    rows = slot_rows
    first = jnp.dot(rows, w_query, preferred_element_type=jnp.float32)
    second = jnp.dot(rows, keyval_flat, preferred_element_type=jnp.float32)
    projected = lax.psum_scatter(
        jnp.concatenate([first, second], 1), "attn", scatter_dimension=0, tiled=True
    )
    my_length = lax.dynamic_slice_in_dim(
        slot_length, lax.axis_index("attn") * req_here, req_here, 0
    )
    position = my_length.astype(jnp.float32)
    queries = rotate(projected[:, :query_cols].reshape(req_here, -1, head_size), position).astype(
        jnp.bfloat16
    )
    fresh = projected[:, query_cols:].reshape(req_here, kv_here, 2 * head_size)
    new_keys = rotate(fresh[..., :head_size], position).astype(jnp.bfloat16)
    new_values = fresh[..., head_size:].astype(jnp.bfloat16)
    all_queries = lax.all_gather(queries.reshape(req_here, query_cols), "grp", axis=1, tiled=True)
    group_size = all_queries.shape[1] // (kv_here * head_size)
    grouped = all_queries.reshape(req_here, kv_here, group_size, head_size)
    scale = head_size ** (-0.5)
    keys_here = cache[..., :head_size]
    values_here = cache[..., head_size:]
    scores = (
        jnp.einsum("rhgd,rhjd->rhgj", grouped, keys_here, preferred_element_type=jnp.float32)
        * scale
    )
    positions = lax.axis_index("grp") * slots_here + jnp.arange(slots_here, dtype=jnp.int32)
    valid = (positions[None, :] < my_length[:, None])[:, None, None, :]
    scores = jnp.where(valid, scores, -1e30)
    top = jnp.max(scores, -1)
    weights = jnp.where(valid, jnp.exp(scores - top[..., None]), 0.0)
    total = jnp.sum(weights, -1)
    mixed = jnp.einsum(
        "rhgj,rhjd->rhgd",
        weights.astype(jnp.bfloat16),
        values_here,
        preferred_element_type=jnp.float32,
    )
    heads_all = kv_here * group_size
    heads_mine = heads_all // grp_count
    top = top.reshape(req_here, heads_all)
    total = total.reshape(req_here, heads_all)
    mixed = mixed.reshape(req_here, heads_all, head_size)
    first_head = lax.axis_index("grp") * heads_mine
    keys_per_head = jnp.repeat(new_keys, group_size, axis=1)
    values_per_head = jnp.repeat(new_values, group_size, axis=1)
    key_mine = lax.dynamic_slice_in_dim(keys_per_head, first_head, heads_mine, 1)
    value_mine = lax.dynamic_slice_in_dim(values_per_head, first_head, heads_mine, 1)
    merged = joined((top, total, mixed), "grp", combine_parts)
    top_mine = lax.dynamic_slice_in_dim(merged[0], first_head, heads_mine, 1)
    total_mine = lax.dynamic_slice_in_dim(merged[1], first_head, heads_mine, 1)
    mixed_mine = lax.dynamic_slice_in_dim(merged[2], first_head, heads_mine, 1)
    attended = finish_heads(top_mine, total_mine, mixed_mine, queries, key_mine, value_mine, scale)
    attended = attended.astype(jnp.bfloat16).reshape(req_here, heads_mine * head_size)
    slot_proj = jnp.dot(
        lax.all_gather(attended, "attn", axis=0, tiled=True),
        w_out,
        preferred_element_type=jnp.float32,
    )
    request_proj = jnp.take(slot_proj, request_slot, axis=0)
    head_total = lax.psum(request_proj, ("ffn", "grp"))
    middle = (resid + head_total).astype(jnp.bfloat16)
    middle_float = middle.astype(jnp.float32)
    squares_ffn = lax.psum(jnp.sum(middle_float * middle_float, axis=1), "attn")
    normed_ffn = (middle_float * lax.rsqrt(squares_ffn / D + 1e-05)[:, None] * gain_ffn).astype(
        jnp.bfloat16
    )
    gate_up_flat = w_gate_up.reshape(w_gate_up.shape[0], -1)
    units = w_gate_up.shape[2]
    rows = normed_ffn
    both = lax.psum_scatter(
        jnp.dot(rows, gate_up_flat, preferred_element_type=jnp.float32),
        "attn",
        scatter_dimension=0,
        tiled=True,
    )
    active = (jax.nn.silu(both[:, :units]) * both[:, units:]).astype(jnp.bfloat16)
    down_part = jnp.dot(
        lax.all_gather(active, "attn", axis=0, tiled=True),
        w_down,
        preferred_element_type=jnp.float32,
    )
    down_total = lax.psum(down_part, ("ffn", "grp"))
    return (middle_float + down_total).astype(jnp.bfloat16)


def solution(mesh):
    placed = (
        P(None, "attn"),
        P("attn"),
        P("attn"),
        P("attn", ("ffn", "grp")),
        P("attn", "ffn", None),
        P(("ffn", "grp"), "attn"),
        P("attn", None, ("ffn", "grp")),
        P(("ffn", "grp"), "attn"),
        P("attn", "ffn", "grp", None),
        P(),
        P(),
    )
    return jax.shard_map(
        shards, mesh=mesh, in_specs=placed, out_specs=P(None, "attn"), check_vma=False
    )
```

profile of v0, /device:TPU:4, one launch (start us, length us, event | category | flops | bytes accessed | tf_op | source)
XLA Modules:
  0.0 1210.6 jit_solution(8739119128693020427)
XLA Ops:
  6.5 0.9 select_reduce_fusion
  7.5 0.7 compare_and_fusion
  8.2 0.9 fusion.9
  9.0 61.7 %psum.28 = f32[64]{0:T(128)S(1)} all-reduce(f32[64]{0:T(128)S(1)} %fusion.9), channel_id=1, replica_groups=mesh['attn'=32,'ffn'=4,'grp'=4] {'attn'}, use_global_device_ids=true, to_apply=%region_3.4 | all-reduce | flops 64 | bytes 512 | tf_op jit(solution)/shard_map/psum | solution.py:71
  70.7 0.8 fusion.11
  71.6 0.7 gather_fusion
  72.3 1.1 fusion.27
  73.5 1.1 fusion.5
  74.6 0.7 pad_maximum_fusion
  75.4 0.7 compare_select_fusion.2
  76.1 1.3 dynamic-slice.2
  78.0 0.1 fusion.54
  78.1 0.1 broadcast_compare_fusion
  78.2 0.1 multiply_cosine_fusion.1
  78.3 265.7 %all-reduce.11.cloned.1.call-done = f32[64,768]{1,0:T(8,128)} async-done(((f32[64,768]{1,0:T(8,128)}), f32[64,768]{1,0:T(8,128)}) %all-reduce.11.cloned.1.call-update) | async-done | bytes 196624
  344.0 0.8 dynamic-slice_bitcast_fusion
  344.7 0.1 fusion.45
  344.9 0.7 constant_dynamic-slice_fusion.2
  345.7 0.1 multiply_subtract_fusion
  345.8 0.2 multiply_reduce_fusion
  345.9 11.1 all_gather.18
  357.0 0.3 fusion.55
  357.3 0.3 fusion.4
  357.6 0.2 fusion.8
  357.8 11.9 all-gather.2
  369.6 8.7 all-gather.4
  378.4 7.2 all-gather.3
  385.6 0.3 while.19
  385.7 0.1 fusion.67
  385.8 0.1 fusion.67
  385.9 0.1 multiply_add_fusion.1
  385.9 0.1 fusion.31
  386.0 41.9 %all-gather.5 = bf16[32,2,512]{2,1,0:T(2,128)(2,1)S(1)} all-gather(bf16[1,2,512]{2,1,0:T(2,128)(2,1)S(1)} %reshape.272), channel_id=1, replica_groups=mesh['attn'=32,'ffn'=4,'grp'=4] {'attn'}, dimensions={0}, use_global_device_ids=true | all-gather | bytes 67584 | tf_op jit(solution)/shard_map/all_gather | solution.py:134
  428.0 0.2 fusion.56
  428.2 0.7 gather_fusion.1
  428.8 0.7 broadcast_select_fusion
  429.6 1.6 copy.20
  431.3 198.1 %all-reduce.7.cloned.1.call-done = f32[64,256]{1,0:T(8,128)} async-done(((f32[64,256]{1,0:T(8,128)}), f32[64,256]{1,0:T(8,128)}) %all-reduce.7.cloned.1.call-update) | async-done | bytes 65552 | tf_op jit(solution)/shard_map/psum | solution.py:139
  629.4 0.9 fusion.13
  630.4 57.7 %psum.30 = f32[64]{0:T(128)S(1)} all-reduce(f32[64]{0:T(128)S(1)} %get-tuple-element.206), channel_id=1, replica_groups=mesh['attn'=32,'ffn'=4,'grp'=4] {'attn'}, use_global_device_ids=true, to_apply=%region_12.13 | all-reduce | flops 64 | bytes 512 | tf_op jit(solution)/shard_map/psum | solution.py:142
  688.1 1.4 fusion.21
  689.5 266.0 %all-reduce.13.cloned.1.call-done = f32[64,3328]{1,0:T(8,128)} async-done(((f32[64,3328]{1,0:T(8,128)}), f32[64,3328]{1,0:T(8,128)}) %all-reduce.13.cloned.1.call-update) | async-done | bytes 851984
  955.6 0.9 fusion.30
  956.5 44.7 %all-gather.6 = bf16[32,2,1664]{2,1,0:T(2,128)(2,1)S(1)} all-gather(bf16[1,2,1664]{2,1,0:T(2,128)(2,1)S(1)} %fusion.30), channel_id=1, replica_groups=mesh['attn'=32,'ffn'=4,'grp'=4] {'attn'}, dimensions={0}, use_global_device_ids=true | all-gather | bytes 219648 | tf_op jit(solution)/shard_map/all_gather | solution.py:157
  1001.2 0.1 reshape.275
  1001.3 0.9 fusion.57
  1002.2 200.3 %all-reduce.9.cloned.1.call-done = f32[64,256]{1,0:T(8,128)} async-done(((f32[64,256]{1,0:T(8,128)}), f32[64,256]{1,0:T(8,128)}) %all-reduce.9.cloned.1.call-update) | async-done | bytes 65552 | tf_op jit(solution)/shard_map/psum | solution.py:161
  1202.6 1.5 fusion.16
  (38 shorter events, 0.5 us)
Async XLA Ops:
  6.5 994.8 %copy-start = (bf16[1664,256]{1,0:T(8,128)(2,1)S(1)}, bf16[1664,256]{1,0:T(8,128)(2,1)}, u32[]{:S(2)}) copy-start(bf16[1664,256]{1,0:T(8,128)(2,1)} %param.20) | copy-start | bytes 2555908
  6.5 350.4 %copy-start.3 = (bf16[2,1,1024,256]{3,2,1,0:T(8,128)(2,1)S(1)}, bf16[2,1,1024,256]{3,2,1,0:T(8,128)(2,1)}, u32[]{:S(2)}) copy-start(bf16[2,1,1024,256]{3,2,1,0:T(8,128)(2,1)} %param.21) | copy-start | bytes 3145732
  6.5 337.4 %all-reduce.11.cloned.1.call-start = ((), (), s32[]{:S(2)}) async-start(), calls=%async_computation.2 | async-start | bytes 393216
  73.5 354.5 %copy-start.2 = (bf16[512,256]{1,0:T(8,128)(2,1)S(1)}, bf16[512,256]{1,0:T(8,128)(2,1)}, u32[]{:S(2)}) copy-start(bf16[512,256]{1,0:T(8,128)(2,1)} %param.18) | copy-start | bytes 786436
  75.3 554.1 %all-reduce.7.cloned.1.call-start = ((), (), s32[]{:S(2)}) async-start(), calls=%async_computation | async-start | bytes 131072 | tf_op jit(solution)/shard_map/psum | solution.py:139
  429.6 526.0 %all-reduce.13.cloned.1.call-start = ((), (), s32[]{:S(2)}) async-start(), calls=%async_computation.3 | async-start | bytes 1703936
  429.6 199.8 %copy-start.1 = (bf16[64,256]{1,0:T(8,128)(2,1)S(1)}, bf16[64,256]{1,0:T(8,128)(2,1)}, u32[]{:S(2)}) copy-start(bf16[64,256]{1,0:T(8,128)(2,1)} %param.13) | copy-start | bytes 98308
  429.6 258.5 %copy-start.4 = (f32[256]{0:T(256)S(1)}, f32[256]{0:T(256)}, u32[]{:S(2)}) copy-start(f32[256]{0:T(256)} %param.15) | copy-start | bytes 3076
  689.5 513.1 %all-reduce.9.cloned.1.call-start = ((), (), s32[]{:S(2)}) async-start(), calls=%async_computation.1 | async-start | bytes 131072 | tf_op jit(solution)/shard_map/psum | solution.py:161
Sparse Core Ops, SparseCore 0:
  75.4 268.4 all-reduce.10
  429.7 199.6 all-reduce.6
  689.6 265.9 all-reduce.12
  1002.3 200.1 all-reduce.8
where the time goes:
time: 1210 us
  waiting for transfers between devices  930 us (77%)
  blocking collectives  245 us (20%)
  between operations  13.9 us (1%)
    unnamed x6, waiting for transfers between devices  532 us
    psum x1, waiting for transfers between devices, shards(): down_total = lax.psum(down_part, ('ffn', 'grp'))  200 us
    psum x1, waiting for transfers between devices, shards(): head_total = lax.psum(request_proj, ('ffn', 'grp'))  198 us
    psum x1, blocking collectives, shards(): squares = lax.psum(jnp.sum(resid * resid, axis=1), 'attn')  61.7 us
    psum x1, blocking collectives, shards(): squares_ffn = lax.psum(jnp.sum(middle_float * middle_float, axis=1), 'attn')  57.7 us
    all_gather x1, blocking collectives, shards(): lax.all_gather(active, 'attn', axis=0, tiled=True)  44.7 us
    all_gather x1, blocking collectives, shards(): lax.all_gather(attended, 'attn', axis=0, tiled=True)  41.9 us
    all_gather x3, blocking collectives, joined(): gathered = jax.tree.map(lambda a: lax.all_gather(a, axis), part)  27.8 us
  transfers between devices with their start and end apart: 4, of which 4 were waited for; matrix products, arithmetic and copies ran while one was open for 0% of the time, Pallas kernels for 0%

commit v1 on v0

v1 whole, which is shorter than its diff:
```python
import jax
import jax.numpy as jnp
from jax import lax
from jax.sharding import PartitionSpec as P

D = 8192
F32 = jnp.float32
BF16 = jnp.bfloat16


def exchange(parts, axis):
    return lax.all_to_all(parts, axis, 0, 0)


def spread(part, axis):
    count = lax.axis_size(axis)
    return exchange(jnp.broadcast_to(part[None], (count,) + part.shape), axis)


def rotate(values, position):
    half = values.shape[-1] // 2
    freqs = 500000.0 ** (-(jnp.arange(half, dtype=F32) * 2.0 / values.shape[-1]))
    angles = position[:, None] * freqs[None, :]
    cosine = jnp.cos(angles)[:, None, :]
    sine = jnp.sin(angles)[:, None, :]
    first = values[..., :half]
    second = values[..., half:]
    return jnp.concatenate([first * cosine - second * sine, second * cosine + first * sine], -1)


def dot(a, b):
    return jnp.dot(a, b, preferred_element_type=F32)


def sum_everywhere(part):
    over_grp = jnp.sum(spread(part.astype(BF16), "grp").astype(F32), 0)
    return jnp.sum(spread(over_grp.astype(BF16), "ffn").astype(F32), 0)


def shards(
    layer_in,
    gain_attn,
    gain_ffn,
    w_query,
    w_keyval,
    w_out,
    w_gate_up,
    w_down,
    cache,
    cache_len,
    request_slot,
):
    requests = layer_in.shape[0]
    req_here = cache.shape[0]
    slots_here = cache.shape[2]
    head_size = cache.shape[3] // 2
    query_cols = w_query.shape[1]
    heads_mine = query_cols // head_size
    attn_count = lax.axis_size("attn")
    grp_count = lax.axis_size("grp")
    heads_all = heads_mine * grp_count
    scale = head_size ** (-0.5)
    order = jnp.arange(requests, dtype=jnp.int32)
    matches = request_slot[None, :] == order[:, None]
    slot_length = jnp.sum(jnp.where(matches, cache_len[None, :], 0), axis=1)
    to_slots = matches.astype(BF16)
    to_requests = (request_slot[:, None] == order[None, :]).astype(BF16)

    resid = layer_in.astype(F32)
    squares = jnp.sum(resid * resid, axis=1)
    squares = jnp.sum(spread(squares[None], "attn"), (0, 1))
    normed = (resid * lax.rsqrt(squares / D + 1e-05)[:, None] * gain_attn).astype(BF16)
    normed = dot(to_slots, normed).astype(BF16)
    weights = jnp.concatenate([w_query, w_keyval.reshape(w_keyval.shape[0], -1)], 1)
    packed = dot(normed, weights)
    summed = jnp.sum(exchange(packed.reshape(attn_count, req_here, -1), "attn"), 0)
    my_length = lax.dynamic_slice_in_dim(
        slot_length, lax.axis_index("attn") * req_here, req_here, 0
    )
    position = my_length.astype(F32)
    queries = rotate(summed[:, :query_cols].reshape(req_here, heads_mine, head_size), position)
    queries = queries.astype(BF16)
    new_key = rotate(summed[:, None, query_cols : query_cols + head_size], position).astype(BF16)
    new_value = summed[:, query_cols + head_size : query_cols + 2 * head_size].astype(BF16)
    all_queries = spread(queries.reshape(req_here, query_cols), "grp")
    grouped = all_queries.reshape(grp_count, req_here, heads_mine, head_size)
    grouped = jnp.swapaxes(grouped, 0, 1).reshape(req_here, heads_all, head_size)

    keys_here = cache[:, 0, :, :head_size]
    values_here = cache[:, 0, :, head_size:]
    scores = jnp.einsum("rgd,rjd->rgj", grouped, keys_here, preferred_element_type=F32) * scale
    positions = lax.axis_index("grp") * slots_here + jnp.arange(slots_here, dtype=jnp.int32)
    valid = (positions[None, :] < my_length[:, None])[:, None, :]
    scores = jnp.where(valid, scores, -1e30)
    top = jnp.max(scores, -1)
    weights = jnp.where(valid, jnp.exp(scores - top[..., None]), 0.0)
    total = jnp.sum(weights, -1)
    mixed = jnp.einsum(
        "rgj,rjd->rgd", weights.astype(BF16), values_here, preferred_element_type=F32
    )
    half = (req_here, heads_all, head_size // 2)
    packed = jnp.concatenate(
        [mixed, jnp.broadcast_to(top[..., None], half), jnp.broadcast_to(total[..., None], half)],
        -1,
    )
    packed = packed.reshape(req_here, grp_count, heads_mine, 2 * head_size)
    packed = exchange(jnp.swapaxes(packed, 0, 1), "grp")
    mixed = packed[..., :head_size]
    top = packed[..., head_size]
    total = packed[..., head_size + head_size // 2]
    own = jnp.sum(queries.astype(F32) * new_key.astype(F32), -1) * scale
    best = jnp.maximum(jnp.max(top, 0), own)
    factor = jnp.exp(top - best)
    own_weight = jnp.exp(own - best)
    denom = jnp.sum(total * factor, 0) + own_weight
    attended = jnp.sum(mixed * factor[..., None], 0)
    attended = attended + own_weight[..., None] * new_value.astype(F32)[:, None, :]
    attended = (attended / denom[..., None]).astype(BF16).reshape(req_here, query_cols)
    attended = spread(attended, "attn").reshape(requests, query_cols)
    attended = dot(to_requests, attended).astype(BF16)
    middle = (resid + sum_everywhere(dot(attended, w_out))).astype(BF16)

    middle_float = middle.astype(F32)
    squares = jnp.sum(middle_float * middle_float, axis=1)
    squares_high = squares.astype(BF16)
    squares_low = (squares - squares_high.astype(F32)).astype(BF16)
    half = (requests, 64)
    units = w_gate_up.shape[2]
    both = dot((middle_float * gain_ffn).astype(BF16), w_gate_up.reshape(w_gate_up.shape[0], -1))
    packed = jnp.concatenate(
        [
            both.astype(BF16),
            jnp.broadcast_to(squares_high[:, None], half),
            jnp.broadcast_to(squares_low[:, None], half),
        ],
        1,
    )
    packed = exchange(packed.reshape(attn_count, req_here, -1), "attn").astype(F32)
    summed = jnp.sum(packed, 0)
    squares = summed[:, 2 * units] + summed[:, 2 * units + 64]
    summed = summed * lax.rsqrt(squares / D + 1e-05)[:, None]
    active = (jax.nn.silu(summed[:, :units]) * summed[:, units : 2 * units]).astype(BF16)
    active = spread(active, "attn").reshape(requests, units)
    return (middle_float + sum_everywhere(dot(active, w_down))).astype(BF16)


def solution(mesh):
    placed = (
        P(None, "attn"),
        P("attn"),
        P("attn"),
        P("attn", ("ffn", "grp")),
        P("attn", "ffn", None),
        P(("ffn", "grp"), "attn"),
        P("attn", None, ("ffn", "grp")),
        P(("ffn", "grp"), "attn"),
        P("attn", "ffn", "grp", None),
        P(),
        P(),
    )
    return jax.shard_map(
        shards, mesh=mesh, in_specs=placed, out_specs=P(None, "attn"), check_vma=False
    )
```

time: 1210 us -> 165 us (0.14)
  the two profiles are of different devices: /device:TPU:4 before, /device:TPU:32 now
where the time goes in v1:
time: 165 us; the launch traced here: 164 us
  blocking collectives  93.5 us (57%)
  waiting for transfers between devices  31.8 us (19%)
  starting transfers between devices  25.1 us (15%)
  local copies, waits for them, and re-layouts  5.29 us (3%)
  other arithmetic  4.82 us (3%)
  matrix products  3.02 us (2%)
    all_to_all x7, blocking collectives, exchange(): return lax.all_to_all(parts, axis, 0, 0)  93.5 us
    all_to_all x4, waiting for transfers between devices, exchange(): return lax.all_to_all(parts, axis, 0, 0)  31.8 us
    all_to_all x4, starting transfers between devices, exchange(): return lax.all_to_all(parts, axis, 0, 0)  25.1 us
  transfers between devices with their start and end apart: 4, of which 4 were waited for; matrix products, arithmetic and copies ran while one was open for 2% of the time, Pallas kernels for 0%

profile of v1, /device:TPU:32, one launch (start us, length us, event | category | flops | bytes accessed | tf_op | source)
XLA Modules:
  0.0 163.8 jit_solution(18013128889575904272)
XLA Ops:
  0.0 1.0 fusion.10
  1.0 14.9 %all_to_all.55 = f32[32,1,64]{2,1,0:T(1,128)S(1)} all-to-all(f32[32,1,64]{2,1,0:T(1,128)S(1)} %broadcast_in_dim.59), channel_id=1, replica_groups=mesh['attn'=32,'ffn'=4,'grp'=4] {'attn'}, dimensions={0} | all-to-all | bytes 16384 | tf_op jit(solution)/shard_map/all_to_all | solution.py:12
  15.9 1.4 fusion.3
  17.4 0.8 reshape.263
  18.2 5.0 %all-to-all-start.1 = ((f32[32,2,768]{2,1,0:T(2,128)}), f32[32,2,768]{2,1,0:T(2,128)S(1)}, u32[]{:S(2)}, u32[]{:S(2)}) async-start(f32[32,2,768]{2,1,0:T(2,128)} %reshape.263), calls=%async_computation.1 | async-start | bytes 393216 | tf_op jit(solution)/shard_map/all_to_all | solution.py:12
  23.2 0.8 select_reduce_fusion
  24.0 0.1 fusion.57
  24.1 0.1 multiply_cosine_fusion.1
  24.2 7.4 %all-to-all-done.1 = f32[32,2,768]{2,1,0:T(2,128)S(1)} async-done(((f32[32,2,768]{2,1,0:T(2,128)}), f32[32,2,768]{2,1,0:T(2,128)S(1)}, u32[]{:S(2)}, u32[]{:S(2)}) %all-to-all-start.1) | async-done | bytes 196640 | tf_op jit(solution)/shard_map/all_to_all | solution.py:12
  31.6 0.1 reduce_sum.135
  31.7 0.1 fusion.51
  32.0 0.2 multiply_reduce_fusion.1
  32.2 0.6 broadcast_in_dim.60
  32.8 4.5 %all-to-all-start.2 = ((bf16[4,2,512]{2,1,0:T(2,128)(2,1)}), bf16[4,2,512]{2,1,0:T(2,128)(2,1)S(1)}, u32[]{:S(2)}, u32[]{:S(2)}) async-start(bf16[4,2,512]{2,1,0:T(2,128)(2,1)} %broadcast_in_dim.60), calls=%async_computation.2 | async-start | bytes 16384 | tf_op jit(solution)/shard_map/all_to_all | solution.py:12
  37.3 5.2 %all-to-all-done.2 = bf16[4,2,512]{2,1,0:T(2,128)(2,1)S(1)} async-done(((bf16[4,2,512]{2,1,0:T(2,128)(2,1)}), bf16[4,2,512]{2,1,0:T(2,128)(2,1)S(1)}, u32[]{:S(2)}, u32[]{:S(2)}) %all-to-all-start.2) | async-done | bytes 8224 | tf_op jit(solution)/shard_map/all_to_all | solution.py:12
  42.6 0.3 fusion.58
  42.9 0.3 fusion.4
  43.2 0.2 fusion.8
  43.5 0.1 pad_maximum_fusion
  43.6 0.6 copy.58
  44.3 3.3 %all-to-all-start.3 = ((f32[4,2,4,256]{3,2,1,0:T(4,128)}), f32[4,2,4,256]{3,2,1,0:T(4,128)S(1)}, u32[]{:S(2)}, u32[]{:S(2)}) async-start(f32[4,2,4,256]{3,2,1,0:T(4,128)} %bitcast.38), calls=%async_computation.3 | async-start | bytes 65536 | tf_op jit(solution)/shard_map/all_to_all | solution.py:12
  47.5 5.4 %all-to-all-done.3 = f32[4,2,4,256]{3,2,1,0:T(4,128)S(1)} async-done(((f32[4,2,4,256]{3,2,1,0:T(4,128)}), f32[4,2,4,256]{3,2,1,0:T(4,128)S(1)}, u32[]{:S(2)}, u32[]{:S(2)}) %all-to-all-start.3) | async-done | bytes 32800 | tf_op jit(solution)/shard_map/all_to_all | solution.py:12
  52.9 0.1 slice_reduce_fusion.2
  53.0 0.2 exponential_reduce_fusion
  53.3 0.1 fusion.29
  53.4 0.1 fusion.37
  53.5 11.5 %all_to_all.56 = bf16[32,2,512]{2,1,0:T(2,128)(2,1)S(1)} all-to-all(bf16[32,2,512]{2,1,0:T(2,128)(2,1)S(1)} %broadcast_in_dim.66), channel_id=1, replica_groups=mesh['attn'=32,'ffn'=4,'grp'=4] {'attn'}, dimensions={0} | all-to-all | bytes 131072 | tf_op jit(solution)/shard_map/all_to_all | solution.py:12
  65.0 0.3 fusion.2
  65.4 8.4 %all_to_all.57 = bf16[4,64,256]{2,1,0:T(8,128)(2,1)S(1)} all-to-all(bf16[4,64,256]{2,1,0:T(8,128)(2,1)S(1)} %broadcast_in_dim.67), channel_id=1, replica_groups=mesh['attn'=32,'ffn'=4,'grp'=4] {'grp'}, dimensions={0} | all-to-all | bytes 262144 | tf_op jit(solution)/shard_map/all_to_all | solution.py:12
  73.8 0.6 broadcast_in_dim.68
  74.4 12.4 %all-to-all-start.6 = ((bf16[4,64,256]{2,1,0:T(8,128)(2,1)}), bf16[4,64,256]{2,1,0:T(8,128)(2,1)S(1)}, u32[]{:S(2)}, u32[]{:S(2)}) async-start(bf16[4,64,256]{2,1,0:T(8,128)(2,1)} %broadcast_in_dim.68), calls=%async_computation.6 | async-start | bytes 262144 | tf_op jit(solution)/shard_map/all_to_all | solution.py:12
  86.8 1.6 %copy.54 = bf16[32,8,2,1664]{3,1,2,0:T(8,128)(2,1)S(1)} copy(bf16[32,8,2,1664]{3,2,1,0:T(2,128)(2,1)} %bitcast.42) | data formatting | bytes 3407872
  88.5 13.7 %all-to-all-done.6 = bf16[4,64,256]{2,1,0:T(8,128)(2,1)S(1)} async-done(((bf16[4,64,256]{2,1,0:T(8,128)(2,1)}), bf16[4,64,256]{2,1,0:T(8,128)(2,1)S(1)}, u32[]{:S(2)}, u32[]{:S(2)}) %all-to-all-start.6) | async-done | bytes 131104 | tf_op jit(solution)/shard_map/all_to_all | solution.py:12
  102.2 0.1 fusion.15
  102.3 0.4 convolution_convert_fusion
  102.9 0.1 concatenate.31
  103.0 0.2 reshape.270
  103.2 17.7 %all_to_all.58 = bf16[32,2,3456]{2,1,0:T(2,128)(2,1)S(1)} all-to-all(bf16[32,2,3456]{2,1,0:T(2,128)(2,1)S(1)} %reshape.270), channel_id=1, replica_groups=mesh['attn'=32,'ffn'=4,'grp'=4] {'attn'}, dimensions={0} | all-to-all | bytes 884736 | tf_op jit(solution)/shard_map/all_to_all | solution.py:12
  120.9 0.4 convert_reduce_fusion
  121.2 0.2 fusion.47
  121.4 0.1 broadcast_multiply_fusion
  121.5 0.1 broadcast_in_dim.71
  121.7 13.8 %all_to_all.59 = bf16[32,2,1664]{2,1,0:T(2,128)(2,1)S(1)} all-to-all(bf16[32,2,1664]{2,1,0:T(2,128)(2,1)S(1)} %broadcast_in_dim.71), channel_id=1, replica_groups=mesh['attn'=32,'ffn'=4,'grp'=4] {'attn'}, dimensions={0} | all-to-all | bytes 425984 | tf_op jit(solution)/shard_map/all_to_all | solution.py:12
  135.4 0.1 reshape.271
  135.5 0.3 convolution_convert_fusion.2
  135.8 8.4 %all_to_all.60 = bf16[4,64,256]{2,1,0:T(8,128)(2,1)S(1)} all-to-all(bf16[4,64,256]{2,1,0:T(8,128)(2,1)S(1)} %broadcast_in_dim.72), channel_id=1, replica_groups=mesh['attn'=32,'ffn'=4,'grp'=4] {'grp'}, dimensions={0} | all-to-all | bytes 262144 | tf_op jit(solution)/shard_map/all_to_all | solution.py:12
  144.3 18.9 %all_to_all.61 = bf16[4,64,256]{2,1,0:T(8,128)(2,1)S(1)} all-to-all(bf16[4,64,256]{2,1,0:T(8,128)(2,1)S(1)} %broadcast_in_dim.73), channel_id=1, replica_groups=mesh['attn'=32,'ffn'=4,'grp'=4] {'ffn'}, dimensions={0} | all-to-all | bytes 262144 | tf_op jit(solution)/shard_map/all_to_all | solution.py:12
  163.2 0.6 fusion.16
  (47 shorter events, 0.9 us)
Async XLA Ops:
  0.0 135.5 %copy-start = (bf16[1664,256]{1,0:T(8,128)(2,1)S(1)}, bf16[1664,256]{1,0:T(8,128)(2,1)}, u32[]{:S(2)}) copy-start(bf16[1664,256]{1,0:T(8,128)(2,1)} %param.18) | copy-start | bytes 2555908
  0.0 42.6 %copy-start.1 = (bf16[2,1,1024,256]{3,2,1,0:T(8,128)(2,1)S(1)}, bf16[2,1,1024,256]{3,2,1,0:T(8,128)(2,1)}, u32[]{:S(2)}) copy-start(bf16[2,1,1024,256]{3,2,1,0:T(8,128)(2,1)} %param.19) | copy-start | bytes 3145732
  17.4 47.7 %copy-start.2 = (bf16[512,256]{1,0:T(8,128)(2,1)S(1)}, bf16[512,256]{1,0:T(8,128)(2,1)}, u32[]{:S(2)}) copy-start(bf16[512,256]{1,0:T(8,128)(2,1)} %param.16) | copy-start | bytes 786436
  17.4 47.7 %copy-start.5 = (s32[64]{0:T(128)S(1)}, s32[64]{0:T(128)}, u32[]{:S(2)}) copy-start(s32[64]{0:T(128)} %param.21) | copy-start | bytes 772
  18.2 13.5 %all-to-all-start.1 = ((f32[32,2,768]{2,1,0:T(2,128)}), f32[32,2,768]{2,1,0:T(2,128)S(1)}, u32[]{:S(2)}, u32[]{:S(2)}) async-start(f32[32,2,768]{2,1,0:T(2,128)} %reshape.263), calls=%async_computation.1 | async-start | bytes 393216 | tf_op jit(solution)/shard_map/all_to_all | solution.py:12
  32.8 9.8 %all-to-all-start.2 = ((bf16[4,2,512]{2,1,0:T(2,128)(2,1)}), bf16[4,2,512]{2,1,0:T(2,128)(2,1)S(1)}, u32[]{:S(2)}, u32[]{:S(2)}) async-start(bf16[4,2,512]{2,1,0:T(2,128)(2,1)} %broadcast_in_dim.60), calls=%async_computation.2 | async-start | bytes 16384 | tf_op jit(solution)/shard_map/all_to_all | solution.py:12
  44.3 8.7 %all-to-all-start.3 = ((f32[4,2,4,256]{3,2,1,0:T(4,128)}), f32[4,2,4,256]{3,2,1,0:T(4,128)S(1)}, u32[]{:S(2)}, u32[]{:S(2)}) async-start(f32[4,2,4,256]{3,2,1,0:T(4,128)} %bitcast.38), calls=%async_computation.3 | async-start | bytes 65536 | tf_op jit(solution)/shard_map/all_to_all | solution.py:12
  74.4 27.7 %all-to-all-start.6 = ((bf16[4,64,256]{2,1,0:T(8,128)(2,1)}), bf16[4,64,256]{2,1,0:T(8,128)(2,1)S(1)}, u32[]{:S(2)}, u32[]{:S(2)}) async-start(bf16[4,64,256]{2,1,0:T(8,128)(2,1)} %broadcast_in_dim.68), calls=%async_computation.6 | async-start | bytes 262144 | tf_op jit(solution)/shard_map/all_to_all | solution.py:12
  86.8 15.3 %copy-start.3 = (bf16[64,256]{1,0:T(8,128)(2,1)S(1)}, bf16[64,256]{1,0:T(8,128)(2,1)}, u32[]{:S(2)}) copy-start(bf16[64,256]{1,0:T(8,128)(2,1)} %param.11) | copy-start | bytes 98308
  86.8 15.5 %copy-start.4 = (f32[256]{0:T(256)S(1)}, f32[256]{0:T(256)}, u32[]{:S(2)}) copy-start(f32[256]{0:T(256)} %param.13) | copy-start | bytes 3076

commit v2 on v1

--- a/solution.py
+++ b/solution.py
@@ -17,12 +17,15 @@
     return exchange(jnp.broadcast_to(part[None], (count,) + part.shape), axis)
 
 
-def rotate(values, position):
+def angles(position, size):
+    half = size // 2
+    freqs = 500000.0 ** (-(jnp.arange(half, dtype=F32) * 2.0 / size))
+    turned = position[:, None] * freqs[None, :]
+    return jnp.cos(turned)[:, None, :], jnp.sin(turned)[:, None, :]
+
+
+def rotate(values, cosine, sine):
     half = values.shape[-1] // 2
-    freqs = 500000.0 ** (-(jnp.arange(half, dtype=F32) * 2.0 / values.shape[-1]))
-    angles = position[:, None] * freqs[None, :]
-    cosine = jnp.cos(angles)[:, None, :]
-    sine = jnp.sin(angles)[:, None, :]
     first = values[..., :half]
     second = values[..., half:]
     return jnp.concatenate([first * cosine - second * sine, second * cosine + first * sine], -1)
@@ -62,35 +65,50 @@
     scale = head_size ** (-0.5)
     order = jnp.arange(requests, dtype=jnp.int32)
     matches = request_slot[None, :] == order[:, None]
+    slot_rows = dot(matches.astype(BF16), layer_in)
+    squares = jnp.sum(slot_rows * slot_rows, axis=1)
+    squares = spread(squares[None], "attn")
+
     slot_length = jnp.sum(jnp.where(matches, cache_len[None, :], 0), axis=1)
-    to_slots = matches.astype(BF16)
-    to_requests = (request_slot[:, None] == order[None, :]).astype(BF16)
-
-    resid = layer_in.astype(F32)
-    squares = jnp.sum(resid * resid, axis=1)
-    squares = jnp.sum(spread(squares[None], "attn"), (0, 1))
-    normed = (resid * lax.rsqrt(squares / D + 1e-05)[:, None] * gain_attn).astype(BF16)
-    normed = dot(to_slots, normed).astype(BF16)
-    weights = jnp.concatenate([w_query, w_keyval.reshape(w_keyval.shape[0], -1)], 1)
-    packed = dot(normed, weights)
-    summed = jnp.sum(exchange(packed.reshape(attn_count, req_here, -1), "attn"), 0)
     my_length = lax.dynamic_slice_in_dim(
         slot_length, lax.axis_index("attn") * req_here, req_here, 0
     )
-    position = my_length.astype(F32)
-    queries = rotate(summed[:, :query_cols].reshape(req_here, heads_mine, head_size), position)
+    cosine, sine = angles(my_length.astype(F32), head_size)
+    positions = lax.axis_index("grp") * slots_here + jnp.arange(slots_here, dtype=jnp.int32)
+    valid = (positions[None, :] < my_length[:, None])[:, None, :]
+    share = 2 * head_size // grp_count
+    keyval_share = lax.dynamic_slice_in_dim(
+        w_keyval[:, 0, :], lax.axis_index("grp") * share, share, 1
+    )
+    weights = jnp.concatenate([w_query, keyval_share], 1)
+    gate_up = w_gate_up.reshape(w_gate_up.shape[0], -1)
+    squares, cosine, sine, valid, weights, gate_up, slot_rows = lax.optimization_barrier(
+        (squares, cosine, sine, valid, weights, gate_up, slot_rows)
+    )
+    squares = jnp.sum(squares, (0, 1))
+    normed = (slot_rows * lax.rsqrt(squares / D + 1e-05)[:, None] * gain_attn).astype(BF16)
+    packed = dot(normed, weights)
+    summed = jnp.sum(exchange(packed.reshape(attn_count, req_here, -1), "attn"), 0)
+    queries = rotate(
+        summed[:, :query_cols].reshape(req_here, heads_mine, head_size), cosine, sine
+    )
     queries = queries.astype(BF16)
-    new_key = rotate(summed[:, None, query_cols : query_cols + head_size], position).astype(BF16)
-    new_value = summed[:, query_cols + head_size : query_cols + 2 * head_size].astype(BF16)
-    all_queries = spread(queries.reshape(req_here, query_cols), "grp")
+    sent = jnp.concatenate(
+        [queries.astype(F32).reshape(req_here, query_cols), summed[:, query_cols:]], 1
+    )
+    arrived = spread(sent, "grp")
+    fresh = jnp.swapaxes(arrived[..., query_cols:], 0, 1).reshape(req_here, 2 * head_size)
+    new_key = rotate(fresh[:, None, :head_size], cosine, sine).astype(BF16)
+    new_value = fresh[:, head_size:].astype(BF16)
+    own = jnp.sum(queries.astype(F32) * new_key.astype(F32), -1) * scale
+    all_queries = arrived[..., :query_cols].astype(BF16)
+    new_value, own, all_queries = lax.optimization_barrier((new_value, own, all_queries))
     grouped = all_queries.reshape(grp_count, req_here, heads_mine, head_size)
     grouped = jnp.swapaxes(grouped, 0, 1).reshape(req_here, heads_all, head_size)
 
     keys_here = cache[:, 0, :, :head_size]
     values_here = cache[:, 0, :, head_size:]
     scores = jnp.einsum("rgd,rjd->rgj", grouped, keys_here, preferred_element_type=F32) * scale
-    positions = lax.axis_index("grp") * slots_here + jnp.arange(slots_here, dtype=jnp.int32)
-    valid = (positions[None, :] < my_length[:, None])[:, None, :]
     scores = jnp.where(valid, scores, -1e30)
     top = jnp.max(scores, -1)
     weights = jnp.where(valid, jnp.exp(scores - top[..., None]), 0.0)
@@ -108,7 +126,6 @@
     mixed = packed[..., :head_size]
     top = packed[..., head_size]
     total = packed[..., head_size + head_size // 2]
-    own = jnp.sum(queries.astype(F32) * new_key.astype(F32), -1) * scale
     best = jnp.maximum(jnp.max(top, 0), own)
     factor = jnp.exp(top - best)
     own_weight = jnp.exp(own - best)
@@ -117,7 +134,9 @@
     attended = attended + own_weight[..., None] * new_value.astype(F32)[:, None, :]
     attended = (attended / denom[..., None]).astype(BF16).reshape(req_here, query_cols)
     attended = spread(attended, "attn").reshape(requests, query_cols)
+    to_requests = (request_slot[:, None] == order[None, :]).astype(BF16)
     attended = dot(to_requests, attended).astype(BF16)
+    resid = layer_in.astype(F32)
     middle = (resid + sum_everywhere(dot(attended, w_out))).astype(BF16)
 
     middle_float = middle.astype(F32)
@@ -126,7 +145,7 @@
     squares_low = (squares - squares_high.astype(F32)).astype(BF16)
     half = (requests, 64)
     units = w_gate_up.shape[2]
-    both = dot((middle_float * gain_ffn).astype(BF16), w_gate_up.reshape(w_gate_up.shape[0], -1))
+    both = dot((middle_float * gain_ffn).astype(BF16), gate_up)
     packed = jnp.concatenate(
         [
             both.astype(BF16),

time: 165 us -> 164 us (level)
  blocking collectives: 93.5 us -> 129 us
  waiting for transfers between devices: 31.8 us -> 7.22 us
  starting transfers between devices: 25.1 us -> 12.2 us
  matrix products: 3.02 us -> 4.96 us
    all_to_all x7 -> x9, blocking collectives: 93.5 us -> 129 us  [exchange(): return lax.all_to_all(parts, axis, 0, 0)]
    all_to_all x4 -> x2, waiting for transfers between devices: 31.8 us -> 7.22 us  [exchange(): return lax.all_to_all(parts, axis, 0, 0)]
    all_to_all x4 -> x2, starting transfers between devices: 25.1 us -> 12.2 us  [exchange(): return lax.all_to_all(parts, axis, 0, 0)]
  transfers between devices with their start and end apart: 4 -> 2, of which waited for: 4 -> 2; matrix products, arithmetic and copies ran while one was open for 2% -> 3% of each run, Pallas kernels for 0% -> 0%
where the time goes in v2:
time: 164 us; the launch traced here: 163 us
  blocking collectives  129 us (79%)
  starting transfers between devices  12.2 us (7%)
  waiting for transfers between devices  7.22 us (4%)
  local copies, waits for them, and re-layouts  5.01 us (3%)
  matrix products  4.96 us (3%)
  other arithmetic  4.82 us (3%)
    all_to_all x9, blocking collectives, exchange(): return lax.all_to_all(parts, axis, 0, 0)  129 us
    all_to_all x2, starting transfers between devices, exchange(): return lax.all_to_all(parts, axis, 0, 0)  12.2 us
    all_to_all x2, waiting for transfers between devices, exchange(): return lax.all_to_all(parts, axis, 0, 0)  7.22 us
  transfers between devices with their start and end apart: 2, of which 2 were waited for; matrix products, arithmetic and copies ran while one was open for 3% of the time, Pallas kernels for 0%

profile of v2, /device:TPU:32, one launch (start us, length us, event | category | flops | bytes accessed | tf_op | source)
XLA Modules:
  0.0 163.4 jit_solution(10406626260771496130)
XLA Ops:
  0.0 1.1 multiply_reduce_fusion
  1.1 0.6 broadcast_in_dim.58
  1.7 9.0 %all-to-all-start = ((f32[32,1,64]{2,1,0:T(1,128)}), f32[32,1,64]{2,1,0:T(1,128)S(1)}, u32[]{:S(2)}, u32[]{:S(2)}) async-start(f32[32,1,64]{2,1,0:T(1,128)} %broadcast_in_dim.58), calls=%async_computation | async-start | bytes 32768 | tf_op jit(solution)/shard_map/all_to_all | solution.py:12
  10.7 0.8 select_reduce_fusion
  11.5 0.1 fusion.36
  11.6 0.1 multiply_sine_fusion
  11.8 0.9 dynamic-slice_bitcast_fusion
  12.7 1.0 pad_maximum_fusion
  13.7 1.6 %copy.46 = bf16[32,8,2,1664]{3,1,2,0:T(8,128)(2,1)S(1)} copy(bf16[32,8,2,1664]{3,2,1,0:T(2,128)(2,1)} %bitcast.49) | data formatting | bytes 3407872
  15.4 1.8 %all-to-all-done = f32[32,1,64]{2,1,0:T(1,128)S(1)} async-done(((f32[32,1,64]{2,1,0:T(1,128)}), f32[32,1,64]{2,1,0:T(1,128)S(1)}, u32[]{:S(2)}, u32[]{:S(2)}) %all-to-all-start) | async-done | bytes 8224 | tf_op jit(solution)/shard_map/all_to_all | solution.py:12
  17.2 0.2 fusion.13
  17.5 0.1 reshape.250
  17.6 13.6 %all_to_all.55 = f32[32,2,576]{2,1,0:T(2,128)S(1)} all-to-all(f32[32,2,576]{2,1,0:T(2,128)S(1)} %reshape.250), channel_id=1, replica_groups=mesh['attn'=32,'ffn'=4,'grp'=4] {'attn'}, dimensions={0} | all-to-all | bytes 294912 | tf_op jit(solution)/shard_map/all_to_all | solution.py:12
  31.3 0.1 multiply_subtract_fusion
  31.4 0.1 convert_bitcast_fusion
  31.5 9.2 %all_to_all.56 = f32[4,2,576]{2,1,0:T(2,128)S(1)} all-to-all(f32[4,2,576]{2,1,0:T(2,128)S(1)} %broadcast_in_dim.63), channel_id=1, replica_groups=mesh['attn'=32,'ffn'=4,'grp'=4] {'grp'}, dimensions={0} | all-to-all | bytes 36864 | tf_op jit(solution)/shard_map/all_to_all | solution.py:12
  40.7 0.1 reshape.252
  40.8 0.1 fusion.32
  40.9 0.1 fusion.25
  41.1 1.4 fusion.37
  42.5 0.2 fusion.4
  42.6 1.3 fusion.3
  44.2 0.6 copy.52
  44.8 3.3 %all-to-all-start.3 = ((f32[4,2,4,256]{3,2,1,0:T(4,128)}), f32[4,2,4,256]{3,2,1,0:T(4,128)S(1)}, u32[]{:S(2)}, u32[]{:S(2)}) async-start(f32[4,2,4,256]{3,2,1,0:T(4,128)} %bitcast.45), calls=%async_computation.3 | async-start | bytes 65536 | tf_op jit(solution)/shard_map/all_to_all | solution.py:12
  48.1 5.4 %all-to-all-done.3 = f32[4,2,4,256]{3,2,1,0:T(4,128)S(1)} async-done(((f32[4,2,4,256]{3,2,1,0:T(4,128)}), f32[4,2,4,256]{3,2,1,0:T(4,128)S(1)}, u32[]{:S(2)}, u32[]{:S(2)}) %all-to-all-start.3) | async-done | bytes 32800 | tf_op jit(solution)/shard_map/all_to_all | solution.py:12
  53.5 0.1 slice_reduce_fusion.2
  53.6 0.2 exponential_reduce_fusion
  53.8 0.1 fusion.19
  53.9 0.1 fusion.27
  54.0 11.4 %all_to_all.57 = bf16[32,2,512]{2,1,0:T(2,128)(2,1)S(1)} all-to-all(bf16[32,2,512]{2,1,0:T(2,128)(2,1)S(1)} %broadcast_in_dim.69), channel_id=1, replica_groups=mesh['attn'=32,'ffn'=4,'grp'=4] {'attn'}, dimensions={0} | all-to-all | bytes 131072 | tf_op jit(solution)/shard_map/all_to_all | solution.py:12
  65.5 0.3 fusion.2
  65.9 8.4 %all_to_all.58 = bf16[4,64,256]{2,1,0:T(8,128)(2,1)S(1)} all-to-all(bf16[4,64,256]{2,1,0:T(8,128)(2,1)S(1)} %broadcast_in_dim.70), channel_id=1, replica_groups=mesh['attn'=32,'ffn'=4,'grp'=4] {'grp'}, dimensions={0} | all-to-all | bytes 262144 | tf_op jit(solution)/shard_map/all_to_all | solution.py:12
  74.3 27.5 %all_to_all.59 = bf16[4,64,256]{2,1,0:T(8,128)(2,1)S(1)} all-to-all(bf16[4,64,256]{2,1,0:T(8,128)(2,1)S(1)} %broadcast_in_dim.71), channel_id=1, replica_groups=mesh['attn'=32,'ffn'=4,'grp'=4] {'ffn'}, dimensions={0} | all-to-all | bytes 262144 | tf_op jit(solution)/shard_map/all_to_all | solution.py:12
  101.8 0.1 fusion.7
  102.0 0.4 convolution_convert_fusion
  102.5 0.1 concatenate.35
  102.7 0.2 reshape.257
  102.8 17.7 %all_to_all.60 = bf16[32,2,3456]{2,1,0:T(2,128)(2,1)S(1)} all-to-all(bf16[32,2,3456]{2,1,0:T(2,128)(2,1)S(1)} %reshape.257), channel_id=1, replica_groups=mesh['attn'=32,'ffn'=4,'grp'=4] {'attn'}, dimensions={0} | all-to-all | bytes 884736 | tf_op jit(solution)/shard_map/all_to_all | solution.py:12
  120.5 0.4 convert_reduce_fusion
  120.9 0.2 fusion.31
  121.1 0.1 broadcast_multiply_fusion
  121.2 0.1 broadcast_in_dim.74
  121.3 13.8 %all_to_all.61 = bf16[32,2,1664]{2,1,0:T(2,128)(2,1)S(1)} all-to-all(bf16[32,2,1664]{2,1,0:T(2,128)(2,1)S(1)} %broadcast_in_dim.74), channel_id=1, replica_groups=mesh['attn'=32,'ffn'=4,'grp'=4] {'attn'}, dimensions={0} | all-to-all | bytes 425984 | tf_op jit(solution)/shard_map/all_to_all | solution.py:12
  135.1 0.1 reshape.258
  135.2 0.3 convolution_convert_fusion.2
  135.5 8.4 %all_to_all.62 = bf16[4,64,256]{2,1,0:T(8,128)(2,1)S(1)} all-to-all(bf16[4,64,256]{2,1,0:T(8,128)(2,1)S(1)} %broadcast_in_dim.75), channel_id=1, replica_groups=mesh['attn'=32,'ffn'=4,'grp'=4] {'grp'}, dimensions={0} | all-to-all | bytes 262144 | tf_op jit(solution)/shard_map/all_to_all | solution.py:12
  143.9 18.9 %all_to_all.63 = bf16[4,64,256]{2,1,0:T(8,128)(2,1)S(1)} all-to-all(bf16[4,64,256]{2,1,0:T(8,128)(2,1)S(1)} %broadcast_in_dim.76), channel_id=1, replica_groups=mesh['attn'=32,'ffn'=4,'grp'=4] {'ffn'}, dimensions={0} | all-to-all | bytes 262144 | tf_op jit(solution)/shard_map/all_to_all | solution.py:12
  162.8 0.6 fusion.8
  (56 shorter events, 1.1 us)
Async XLA Ops:
  0.0 135.2 %copy-start = (bf16[1664,256]{1,0:T(8,128)(2,1)S(1)}, bf16[1664,256]{1,0:T(8,128)(2,1)}, u32[]{:S(2)}) copy-start(bf16[1664,256]{1,0:T(8,128)(2,1)} %param.18) | copy-start | bytes 2555908
  1.7 15.5 %all-to-all-start = ((f32[32,1,64]{2,1,0:T(1,128)}), f32[32,1,64]{2,1,0:T(1,128)S(1)}, u32[]{:S(2)}, u32[]{:S(2)}) async-start(f32[32,1,64]{2,1,0:T(1,128)} %broadcast_in_dim.58), calls=%async_computation | async-start | bytes 32768 | tf_op jit(solution)/shard_map/all_to_all | solution.py:12
  13.7 3.5 %copy-start.4 = (f32[256]{0:T(256)S(1)}, f32[256]{0:T(256)}, u32[]{:S(2)}) copy-start(f32[256]{0:T(256)} %param.12) | copy-start | bytes 3076
  17.5 48.1 %copy-start.1 = (bf16[512,256]{1,0:T(8,128)(2,1)S(1)}, bf16[512,256]{1,0:T(8,128)(2,1)}, u32[]{:S(2)}) copy-start(bf16[512,256]{1,0:T(8,128)(2,1)} %param.16) | copy-start | bytes 786436
  17.5 48.0 %copy-start.3 = (s32[64]{0:T(128)S(1)}, s32[64]{0:T(128)}, u32[]{:S(2)}) copy-start(s32[64]{0:T(128)} %param.21) | copy-start | bytes 772
  42.4 59.4 %copy-start.2 = (bf16[64,256]{1,0:T(8,128)(2,1)S(1)}, bf16[64,256]{1,0:T(8,128)(2,1)}, u32[]{:S(2)}) copy-start(bf16[64,256]{1,0:T(8,128)(2,1)} %param.11) | copy-start | bytes 98308
  42.4 59.5 %copy-start.5 = (f32[256]{0:T(256)S(1)}, f32[256]{0:T(256)}, u32[]{:S(2)}) copy-start(f32[256]{0:T(256)} %param.13) | copy-start | bytes 3076
  44.8 8.7 %all-to-all-start.3 = ((f32[4,2,4,256]{3,2,1,0:T(4,128)}), f32[4,2,4,256]{3,2,1,0:T(4,128)S(1)}, u32[]{:S(2)}, u32[]{:S(2)}) async-start(f32[4,2,4,256]{3,2,1,0:T(4,128)} %bitcast.45), calls=%async_computation.3 | async-start | bytes 65536 | tf_op jit(solution)/shard_map/all_to_all | solution.py:12

commit v3 on v2

--- a/solution.py
+++ b/solution.py
@@ -35,9 +35,16 @@
     return jnp.dot(a, b, preferred_element_type=F32)
 
 
-def sum_everywhere(part):
-    over_grp = jnp.sum(spread(part.astype(BF16), "grp").astype(F32), 0)
-    return jnp.sum(spread(over_grp.astype(BF16), "ffn").astype(F32), 0)
+def sum_pairs(total, axis):
+    for pairs in (((0, 1), (2, 3)), ((0, 3), (1, 2))):
+        swaps = [(a, b) for a, b in pairs] + [(b, a) for a, b in pairs]
+        mine = total.astype(BF16)
+        total = mine.astype(F32) + lax.ppermute(mine, axis, swaps).astype(F32)
+    return total
+
+
+def sum_spread(part, axis):
+    return jnp.sum(spread(part.astype(BF16), axis).astype(F32), 0)
 
 
 def shards(
@@ -76,38 +83,32 @@
     cosine, sine = angles(my_length.astype(F32), head_size)
     positions = lax.axis_index("grp") * slots_here + jnp.arange(slots_here, dtype=jnp.int32)
     valid = (positions[None, :] < my_length[:, None])[:, None, :]
-    share = 2 * head_size // grp_count
-    keyval_share = lax.dynamic_slice_in_dim(
-        w_keyval[:, 0, :], lax.axis_index("grp") * share, share, 1
-    )
-    weights = jnp.concatenate([w_query, keyval_share], 1)
-    gate_up = w_gate_up.reshape(w_gate_up.shape[0], -1)
-    squares, cosine, sine, valid, weights, gate_up, slot_rows = lax.optimization_barrier(
-        (squares, cosine, sine, valid, weights, gate_up, slot_rows)
+    keys_here = cache[:, 0, :, :head_size]
+    values_here = cache[:, 0, :, head_size:]
+    weights = jnp.concatenate([w_query, w_keyval.reshape(w_keyval.shape[0], -1)], 1)
+    squares, cosine, sine, valid, keys_here, values_here, weights = lax.optimization_barrier(
+        (squares, cosine, sine, valid, keys_here, values_here, weights)
     )
     squares = jnp.sum(squares, (0, 1))
     normed = (slot_rows * lax.rsqrt(squares / D + 1e-05)[:, None] * gain_attn).astype(BF16)
     packed = dot(normed, weights)
-    summed = jnp.sum(exchange(packed.reshape(attn_count, req_here, -1), "attn"), 0)
+    summed = exchange(packed.reshape(attn_count, req_here, -1), "attn")
+    summed = jnp.sum(summed, 0)
     queries = rotate(
         summed[:, :query_cols].reshape(req_here, heads_mine, head_size), cosine, sine
     )
     queries = queries.astype(BF16)
-    sent = jnp.concatenate(
-        [queries.astype(F32).reshape(req_here, query_cols), summed[:, query_cols:]], 1
+    new_key = rotate(summed[:, None, query_cols : query_cols + head_size], cosine, sine)
+    new_key = new_key.astype(BF16)
+    new_value = summed[:, query_cols + head_size :].astype(BF16).astype(F32)
+    own = jnp.sum(queries.astype(F32) * new_key.astype(F32), -1) * scale
+    flat_queries, new_value, own = lax.optimization_barrier(
+        (queries.reshape(req_here, query_cols), new_value, own)
     )
-    arrived = spread(sent, "grp")
-    fresh = jnp.swapaxes(arrived[..., query_cols:], 0, 1).reshape(req_here, 2 * head_size)
-    new_key = rotate(fresh[:, None, :head_size], cosine, sine).astype(BF16)
-    new_value = fresh[:, head_size:].astype(BF16)
-    own = jnp.sum(queries.astype(F32) * new_key.astype(F32), -1) * scale
-    all_queries = arrived[..., :query_cols].astype(BF16)
-    new_value, own, all_queries = lax.optimization_barrier((new_value, own, all_queries))
+    all_queries = spread(flat_queries, "grp")
     grouped = all_queries.reshape(grp_count, req_here, heads_mine, head_size)
     grouped = jnp.swapaxes(grouped, 0, 1).reshape(req_here, heads_all, head_size)
 
-    keys_here = cache[:, 0, :, :head_size]
-    values_here = cache[:, 0, :, head_size:]
     scores = jnp.einsum("rgd,rjd->rgj", grouped, keys_here, preferred_element_type=F32) * scale
     scores = jnp.where(valid, scores, -1e30)
     top = jnp.max(scores, -1)
@@ -131,13 +132,13 @@
     own_weight = jnp.exp(own - best)
     denom = jnp.sum(total * factor, 0) + own_weight
     attended = jnp.sum(mixed * factor[..., None], 0)
-    attended = attended + own_weight[..., None] * new_value.astype(F32)[:, None, :]
+    attended = attended + own_weight[..., None] * new_value[:, None, :]
     attended = (attended / denom[..., None]).astype(BF16).reshape(req_here, query_cols)
     attended = spread(attended, "attn").reshape(requests, query_cols)
     to_requests = (request_slot[:, None] == order[None, :]).astype(BF16)
     attended = dot(to_requests, attended).astype(BF16)
     resid = layer_in.astype(F32)
-    middle = (resid + sum_everywhere(dot(attended, w_out))).astype(BF16)
+    middle = (resid + sum_pairs(sum_spread(dot(attended, w_out), "grp"), "ffn")).astype(BF16)
 
     middle_float = middle.astype(F32)
     squares = jnp.sum(middle_float * middle_float, axis=1)
@@ -145,7 +146,7 @@
     squares_low = (squares - squares_high.astype(F32)).astype(BF16)
     half = (requests, 64)
     units = w_gate_up.shape[2]
-    both = dot((middle_float * gain_ffn).astype(BF16), gate_up)
+    both = dot((middle_float * gain_ffn).astype(BF16), w_gate_up.reshape(w_gate_up.shape[0], -1))
     packed = jnp.concatenate(
         [
             both.astype(BF16),
@@ -160,7 +161,7 @@
     summed = summed * lax.rsqrt(squares / D + 1e-05)[:, None]
     active = (jax.nn.silu(summed[:, :units]) * summed[:, units : 2 * units]).astype(BF16)
     active = spread(active, "attn").reshape(requests, units)
-    return (middle_float + sum_everywhere(dot(active, w_down))).astype(BF16)
+    return (middle_float + sum_pairs(sum_spread(dot(active, w_down), "grp"), "ffn")).astype(BF16)
 
 
 def solution(mesh):

time: 164 us -> 157 us (0.957)
  the two profiles are of different devices: /device:TPU:32 before, /device:TPU:2 now
where the time goes in v3:
time: 157 us; the launch traced here: 156 us
  blocking collectives  90.3 us (58%)
  starting transfers between devices  40.5 us (26%)
  waiting for transfers between devices  14.9 us (9%)
  other arithmetic  3.84 us (2%)
  local copies, waits for them, and re-layouts  3.19 us (2%)
  matrix products  2.92 us (2%)
    all_to_all x8, blocking collectives, exchange(): return lax.all_to_all(parts, axis, 0, 0)  90.3 us
    ppermute x4, starting transfers between devices, sum_pairs(): total = mine.astype(F32) + lax.ppermute(mine, axis, swaps).astype(F32)  31 us
    ppermute x4, waiting for transfers between devices, sum_pairs(): total = mine.astype(F32) + lax.ppermute(mine, axis, swaps).astype(F32)  10.8 us
    all_to_all x1, starting transfers between devices, exchange(): return lax.all_to_all(parts, axis, 0, 0)  9.43 us
    all_to_all x1, waiting for transfers between devices, exchange(): return lax.all_to_all(parts, axis, 0, 0)  4.1 us
  transfers between devices with their start and end apart: 5, of which 5 were waited for; matrix products, arithmetic and copies ran while one was open for 2% of the time, Pallas kernels for 0%

profile of v3, /device:TPU:2, one launch (start us, length us, event | category | flops | bytes accessed | tf_op | source)
XLA Modules:
  0.0 156.1 jit_solution(6333029507456504573)
XLA Ops:
  0.0 1.1 multiply_reduce_fusion
  1.1 0.6 broadcast_in_dim.54
  1.8 9.4 %all-to-all-start = ((f32[32,1,64]{2,1,0:T(1,128)}), f32[32,1,64]{2,1,0:T(1,128)S(1)}, u32[]{:S(2)}, u32[]{:S(2)}) async-start(f32[32,1,64]{2,1,0:T(1,128)} %broadcast_in_dim.54), calls=%async_computation | async-start | bytes 32768 | tf_op jit(solution)/shard_map/all_to_all | solution.py:12
  11.2 0.8 select_reduce_fusion
  12.0 1.3 slice_bitcast_fusion
  13.3 0.1 fusion.36
  13.5 0.1 multiply_sine_fusion
  13.6 4.1 %all-to-all-done = f32[32,1,64]{2,1,0:T(1,128)S(1)} async-done(((f32[32,1,64]{2,1,0:T(1,128)}), f32[32,1,64]{2,1,0:T(1,128)S(1)}, u32[]{:S(2)}, u32[]{:S(2)}) %all-to-all-start) | async-done | bytes 8224 | tf_op jit(solution)/shard_map/all_to_all | solution.py:12
  17.8 0.2 fusion.13
  18.0 0.1 reshape.245
  18.1 12.7 %all_to_all.45 = f32[32,2,768]{2,1,0:T(2,128)S(1)} all-to-all(f32[32,2,768]{2,1,0:T(2,128)S(1)} %reshape.245), channel_id=1, replica_groups=mesh['attn'=32,'ffn'=4,'grp'=4] {'attn'}, dimensions={0} | all-to-all | bytes 393216 | tf_op jit(solution)/shard_map/all_to_all | solution.py:12
  30.8 0.1 reduce_sum.117
  31.2 0.2 multiply_reduce_fusion.2
  31.4 9.1 %all_to_all.46 = bf16[4,2,512]{2,1,0:T(2,128)(2,1)S(1)} all-to-all(bf16[4,2,512]{2,1,0:T(2,128)(2,1)S(1)} %broadcast_in_dim.60), channel_id=1, replica_groups=mesh['attn'=32,'ffn'=4,'grp'=4] {'grp'}, dimensions={0} | all-to-all | bytes 16384 | tf_op jit(solution)/shard_map/all_to_all | solution.py:12
  40.5 0.3 fusion.37
  40.9 0.2 fusion.3
  41.0 0.3 fusion.8
  41.6 7.8 %all_to_all.47 = f32[4,2,4,256]{3,2,1,0:T(4,128)S(1)} all-to-all(f32[4,2,4,256]{3,2,1,0:T(4,128)S(1)} %bitcast.43), channel_id=1, replica_groups=mesh['attn'=32,'ffn'=4,'grp'=4] {'grp'}, dimensions={0} | all-to-all | bytes 65536 | tf_op jit(solution)/shard_map/all_to_all | solution.py:12
  49.4 0.1 slice_reduce_fusion.2
  49.5 0.2 exponential_reduce_fusion
  49.7 0.1 fusion.19
  49.8 0.1 fusion.26
  49.9 11.5 %all_to_all.48 = bf16[32,2,512]{2,1,0:T(2,128)(2,1)S(1)} all-to-all(bf16[32,2,512]{2,1,0:T(2,128)(2,1)S(1)} %broadcast_in_dim.65), channel_id=1, replica_groups=mesh['attn'=32,'ffn'=4,'grp'=4] {'attn'}, dimensions={0} | all-to-all | bytes 131072 | tf_op jit(solution)/shard_map/all_to_all | solution.py:12
  61.5 0.3 fusion.2
  61.8 8.4 %all_to_all.49 = bf16[4,64,256]{2,1,0:T(8,128)(2,1)S(1)} all-to-all(bf16[4,64,256]{2,1,0:T(8,128)(2,1)S(1)} %broadcast_in_dim.66), channel_id=1, replica_groups=mesh['attn'=32,'ffn'=4,'grp'=4] {'grp'}, dimensions={0} | all-to-all | bytes 262144 | tf_op jit(solution)/shard_map/all_to_all | solution.py:12
  70.2 9.1 %collective-permute-start = (bf16[64,256]{1,0:T(8,128)(2,1)S(1)}, bf16[64,256]{1,0:T(8,128)(2,1)S(1)}, u32[]{:S(2)}, u32[]{:S(2)}) collective-permute-start(bf16[64,256]{1,0:T(8,128)(2,1)S(1)} %reduce_sum.122), channel_id=1, source_target_pairs={{0,4},{8,12},{4,0},{12,8},{1,5},{9,13},{5,1},{13,9},{2,6},{10,14},... | collective-permute-start | bytes 98312 | tf_op jit(solution)/shard_map/ppermute | solution.py:42
  79.3 2.7 %collective-permute-done = bf16[64,256]{1,0:T(8,128)(2,1)S(1)} collective-permute-done((bf16[64,256]{1,0:T(8,128)(2,1)S(1)}, bf16[64,256]{1,0:T(8,128)(2,1)S(1)}, u32[]{:S(2)}, u32[]{:S(2)}) %collective-permute-start) | collective-permute-done | bytes 32800 | tf_op jit(solution)/shard_map/ppermute | solution.py:42
  82.0 8.0 %collective-permute-start.1 = (bf16[64,256]{1,0:T(8,128)(2,1)S(1)}, bf16[64,256]{1,0:T(8,128)(2,1)S(1)}, u32[]{:S(2)}, u32[]{:S(2)}) collective-permute-start(bf16[64,256]{1,0:T(8,128)(2,1)S(1)} %add_convert_fusion.2), channel_id=1, source_target_pairs={{0,12},{4,8},{12,0},{8,4},{1,13},{5,9},{13,1},{9,5},{2,14},{6,10},... | collective-permute-start | bytes 98312 | tf_op jit(solution)/shard_map/ppermute | solution.py:42
  90.0 0.2 copy.35
  90.2 1.7 %collective-permute-done.1 = bf16[64,256]{1,0:T(8,128)(2,1)S(1)} collective-permute-done((bf16[64,256]{1,0:T(8,128)(2,1)S(1)}, bf16[64,256]{1,0:T(8,128)(2,1)S(1)}, u32[]{:S(2)}, u32[]{:S(2)}) %collective-permute-start.1) | collective-permute-done | bytes 32800 | tf_op jit(solution)/shard_map/ppermute | solution.py:42
  91.9 0.1 fusion.6
  92.0 0.4 convolution_convert_fusion
  92.6 0.1 concatenate.31
  92.7 0.2 reshape.252
  92.9 17.3 %all_to_all.50 = bf16[32,2,3456]{2,1,0:T(2,128)(2,1)S(1)} all-to-all(bf16[32,2,3456]{2,1,0:T(2,128)(2,1)S(1)} %reshape.252), channel_id=1, replica_groups=mesh['attn'=32,'ffn'=4,'grp'=4] {'attn'}, dimensions={0} | all-to-all | bytes 884736 | tf_op jit(solution)/shard_map/all_to_all | solution.py:12
  110.2 0.4 convert_reduce_fusion
  110.6 0.2 fusion.30
  110.8 0.1 broadcast_multiply_fusion
  110.9 0.1 broadcast_in_dim.69
  111.0 14.8 %all_to_all.51 = bf16[32,2,1664]{2,1,0:T(2,128)(2,1)S(1)} all-to-all(bf16[32,2,1664]{2,1,0:T(2,128)(2,1)S(1)} %broadcast_in_dim.69), channel_id=1, replica_groups=mesh['attn'=32,'ffn'=4,'grp'=4] {'attn'}, dimensions={0} | all-to-all | bytes 425984 | tf_op jit(solution)/shard_map/all_to_all | solution.py:12
  125.8 0.1 reshape.253
  125.9 0.3 convolution_convert_fusion.2
  126.2 8.7 %all_to_all.52 = bf16[4,64,256]{2,1,0:T(8,128)(2,1)S(1)} all-to-all(bf16[4,64,256]{2,1,0:T(8,128)(2,1)S(1)} %broadcast_in_dim.70), channel_id=1, replica_groups=mesh['attn'=32,'ffn'=4,'grp'=4] {'grp'}, dimensions={0} | all-to-all | bytes 262144 | tf_op jit(solution)/shard_map/all_to_all | solution.py:12
  135.0 7.0 %collective-permute-start.2 = (bf16[64,256]{1,0:T(8,128)(2,1)S(1)}, bf16[64,256]{1,0:T(8,128)(2,1)S(1)}, u32[]{:S(2)}, u32[]{:S(2)}) collective-permute-start(bf16[64,256]{1,0:T(8,128)(2,1)S(1)} %reduce_sum.125), channel_id=1, source_target_pairs={{0,4},{8,12},{4,0},{12,8},{1,5},{9,13},{5,1},{13,9},{2,6},{10,14},... | collective-permute-start | bytes 98312 | tf_op jit(solution)/shard_map/ppermute | solution.py:42
  142.0 3.7 %collective-permute-done.2 = bf16[64,256]{1,0:T(8,128)(2,1)S(1)} collective-permute-done((bf16[64,256]{1,0:T(8,128)(2,1)S(1)}, bf16[64,256]{1,0:T(8,128)(2,1)S(1)}, u32[]{:S(2)}, u32[]{:S(2)}) %collective-permute-start.2) | collective-permute-done | bytes 32800 | tf_op jit(solution)/shard_map/ppermute | solution.py:42
  145.7 7.0 %collective-permute-start.3 = (bf16[64,256]{1,0:T(8,128)(2,1)S(1)}, bf16[64,256]{1,0:T(8,128)(2,1)S(1)}, u32[]{:S(2)}, u32[]{:S(2)}) collective-permute-start(bf16[64,256]{1,0:T(8,128)(2,1)S(1)} %add_convert_fusion), channel_id=1, source_target_pairs={{0,12},{4,8},{12,0},{8,4},{1,13},{5,9},{13,1},{9,5},{2,14},{6,10},... | collective-permute-start | bytes 98312 | tf_op jit(solution)/shard_map/ppermute | solution.py:42
  152.7 2.8 %collective-permute-done.3 = bf16[64,256]{1,0:T(8,128)(2,1)S(1)} collective-permute-done((bf16[64,256]{1,0:T(8,128)(2,1)S(1)}, bf16[64,256]{1,0:T(8,128)(2,1)S(1)}, u32[]{:S(2)}, u32[]{:S(2)}) %collective-permute-start.3) | collective-permute-done | bytes 32800 | tf_op jit(solution)/shard_map/ppermute | solution.py:42
  155.4 0.6 fusion.7
  (57 shorter events, 1.1 us)
Async XLA Ops:
  0.0 125.9 %copy-start = (bf16[1664,256]{1,0:T(8,128)(2,1)S(1)}, bf16[1664,256]{1,0:T(8,128)(2,1)}, u32[]{:S(2)}) copy-start(bf16[1664,256]{1,0:T(8,128)(2,1)} %param.18) | copy-start | bytes 2555908
  0.0 13.6 %copy-start.5 = (bf16[256,1,256]{2,0,1:T(8,128)(2,1)S(1)}, bf16[256,1,256]{2,0,1:T(8,128)(2,1)}, u32[]{:S(2)}) copy-start(bf16[256,1,256]{2,0,1:T(8,128)(2,1)} %param.15) | copy-start | bytes 393220
  0.0 13.6 %copy-start.2 = (bf16[256,512]{1,0:T(8,128)(2,1)S(1)}, bf16[256,512]{1,0:T(8,128)(2,1)}, u32[]{:S(2)}) copy-start(bf16[256,512]{1,0:T(8,128)(2,1)} %param.14) | copy-start | bytes 786436
  0.0 17.8 %copy-start.7 = (f32[256]{0:T(256)S(1)}, f32[256]{0:T(256)}, u32[]{:S(2)}) copy-start(f32[256]{0:T(256)} %param.12) | copy-start | bytes 3076
  1.8 16.0 %all-to-all-start = ((f32[32,1,64]{2,1,0:T(1,128)}), f32[32,1,64]{2,1,0:T(1,128)S(1)}, u32[]{:S(2)}, u32[]{:S(2)}) async-start(f32[32,1,64]{2,1,0:T(1,128)} %broadcast_in_dim.54), calls=%async_computation | async-start | bytes 32768 | tf_op jit(solution)/shard_map/all_to_all | solution.py:12
  18.0 43.4 %copy-start.3 = (bf16[512,256]{1,0:T(8,128)(2,1)S(1)}, bf16[512,256]{1,0:T(8,128)(2,1)}, u32[]{:S(2)}) copy-start(bf16[512,256]{1,0:T(8,128)(2,1)} %param.16) | copy-start | bytes 786436
  18.0 43.4 %copy-start.6 = (s32[64]{0:T(128)S(1)}, s32[64]{0:T(128)}, u32[]{:S(2)}) copy-start(s32[64]{0:T(128)} %param.21) | copy-start | bytes 772
  40.9 49.1 %copy-start.1 = (bf16[256,2,1664]{2,1,0:T(2,128)(2,1)S(1)}, bf16[256,2,1664]{2,1,0:T(2,128)(2,1)}, u32[]{:S(2)}) copy-start(bf16[256,2,1664]{2,1,0:T(2,128)(2,1)} %param.17) | copy-start | bytes 5111812
  70.2 11.8 %collective-permute-start = (bf16[64,256]{1,0:T(8,128)(2,1)S(1)}, bf16[64,256]{1,0:T(8,128)(2,1)S(1)}, u32[]{:S(2)}, u32[]{:S(2)}) collective-permute-start(bf16[64,256]{1,0:T(8,128)(2,1)S(1)} %reduce_sum.122), channel_id=1, source_target_pairs={{0,4},{8,12},{4,0},{12,8},{1,5},{9,13},{5,1},{13,9},{2,6},{10,14},... | collective-permute-start | bytes 98312 | tf_op jit(solution)/shard_map/ppermute | solution.py:42
  82.0 9.9 %collective-permute-start.1 = (bf16[64,256]{1,0:T(8,128)(2,1)S(1)}, bf16[64,256]{1,0:T(8,128)(2,1)S(1)}, u32[]{:S(2)}, u32[]{:S(2)}) collective-permute-start(bf16[64,256]{1,0:T(8,128)(2,1)S(1)} %add_convert_fusion.2), channel_id=1, source_target_pairs={{0,12},{4,8},{12,0},{8,4},{1,13},{5,9},{13,1},{9,5},{2,14},{6,10},... | collective-permute-start | bytes 98312 | tf_op jit(solution)/shard_map/ppermute | solution.py:42
  90.0 1.9 %copy-start.4 = (bf16[64,256]{1,0:T(8,128)(2,1)S(1)}, bf16[64,256]{1,0:T(8,128)(2,1)}, u32[]{:S(2)}) copy-start(bf16[64,256]{1,0:T(8,128)(2,1)} %param.11) | copy-start | bytes 98308
  90.0 2.0 %copy-start.8 = (f32[256]{0:T(256)S(1)}, f32[256]{0:T(256)}, u32[]{:S(2)}) copy-start(f32[256]{0:T(256)} %param.13) | copy-start | bytes 3076
  135.0 10.7 %collective-permute-start.2 = (bf16[64,256]{1,0:T(8,128)(2,1)S(1)}, bf16[64,256]{1,0:T(8,128)(2,1)S(1)}, u32[]{:S(2)}, u32[]{:S(2)}) collective-permute-start(bf16[64,256]{1,0:T(8,128)(2,1)S(1)} %reduce_sum.125), channel_id=1, source_target_pairs={{0,4},{8,12},{4,0},{12,8},{1,5},{9,13},{5,1},{13,9},{2,6},{10,14},... | collective-permute-start | bytes 98312 | tf_op jit(solution)/shard_map/ppermute | solution.py:42
  145.7 9.7 %collective-permute-start.3 = (bf16[64,256]{1,0:T(8,128)(2,1)S(1)}, bf16[64,256]{1,0:T(8,128)(2,1)S(1)}, u32[]{:S(2)}, u32[]{:S(2)}) collective-permute-start(bf16[64,256]{1,0:T(8,128)(2,1)S(1)} %add_convert_fusion), channel_id=1, source_target_pairs={{0,12},{4,8},{12,0},{8,4},{1,13},{5,9},{13,1},{9,5},{2,14},{6,10},... | collective-permute-start | bytes 98312 | tf_op jit(solution)/shard_map/ppermute | solution.py:42

commit v4 on v3

--- a/solution.py
+++ b/solution.py
@@ -35,12 +35,28 @@
     return jnp.dot(a, b, preferred_element_type=F32)
 
 
-def sum_pairs(total, axis):
-    for pairs in (((0, 1), (2, 3)), ((0, 3), (1, 2))):
-        swaps = [(a, b) for a, b in pairs] + [(b, a) for a, b in pairs]
-        mine = total.astype(BF16)
-        total = mine.astype(F32) + lax.ppermute(mine, axis, swaps).astype(F32)
-    return total
+def sum_relay(part, axis, ahead, behind):
+    def swap(values, pair):
+        return lax.ppermute(values, axis, (pair, pair[::-1]))
+
+    def hand(values, sources, targets):
+        return lax.ppermute(values, axis, tuple(zip(sources, targets)))
+
+    def add(one, two):
+        return (one.astype(F32) + two.astype(F32)).astype(BF16)
+
+    mine = part.astype(BF16)
+    from_ahead = swap(mine, ahead)
+    sum_ahead = add(mine, from_ahead)
+    here = (lax.axis_index(axis) == ahead[0]) | (lax.axis_index(axis) == ahead[1])
+    down = hand(jnp.pad(sum_ahead, ((0, 16), (0, 0))), ahead, behind)[: part.shape[0]]
+    mine = jnp.where(here, sum_ahead, mine)
+    from_behind = swap(mine, behind)
+    sum_behind = add(mine, from_behind)
+    up = hand(jnp.where(here, down, sum_behind), behind, ahead)
+    near = jnp.where(here, sum_ahead, sum_behind)
+    far = jnp.where(here, up, down)
+    return near.astype(F32) + far.astype(F32)
 
 
 def sum_spread(part, axis):
@@ -138,7 +154,8 @@
     to_requests = (request_slot[:, None] == order[None, :]).astype(BF16)
     attended = dot(to_requests, attended).astype(BF16)
     resid = layer_in.astype(F32)
-    middle = (resid + sum_pairs(sum_spread(dot(attended, w_out), "grp"), "ffn")).astype(BF16)
+    projected = sum_spread(dot(attended, w_out), "grp")
+    middle = (resid + sum_relay(projected, "ffn", (0, 1), (3, 2))).astype(BF16)
 
     middle_float = middle.astype(F32)
     squares = jnp.sum(middle_float * middle_float, axis=1)
@@ -161,7 +178,8 @@
     summed = summed * lax.rsqrt(squares / D + 1e-05)[:, None]
     active = (jax.nn.silu(summed[:, :units]) * summed[:, units : 2 * units]).astype(BF16)
     active = spread(active, "attn").reshape(requests, units)
-    return (middle_float + sum_pairs(sum_spread(dot(active, w_down), "grp"), "ffn")).astype(BF16)
+    down = sum_spread(dot(active, w_down), "grp")
+    return (middle_float + sum_relay(down, "ffn", (3, 2), (0, 1))).astype(BF16)
 
 
 def solution(mesh):

time: 157 us -> 155 us (0.987)
  the two profiles are of different devices: /device:TPU:2 before, /device:TPU:128 now
where the time goes in v4:
time: 155 us; the launch traced here: 154 us
  blocking collectives  90 us (58%)
  waiting for transfers between devices  34.5 us (22%)
  starting transfers between devices  19.4 us (13%)
  other arithmetic  3.91 us (3%)
  local copies, waits for them, and re-layouts  3.2 us (2%)
  matrix products  2.92 us (2%)
    all_to_all x8, blocking collectives, exchange(): return lax.all_to_all(parts, axis, 0, 0)  90 us
    ppermute x4, waiting for transfers between devices, swap(): return lax.ppermute(values, axis, (pair, pair[::-1]))  15.9 us
    ppermute x4, waiting for transfers between devices, hand(): return lax.ppermute(values, axis, tuple(zip(sources, targets)))  13.4 us
    all_to_all x1, starting transfers between devices, exchange(): return lax.all_to_all(parts, axis, 0, 0)  8.75 us
    ppermute x4, starting transfers between devices, hand(): return lax.ppermute(values, axis, tuple(zip(sources, targets)))  5.36 us
    ppermute x4, starting transfers between devices, swap(): return lax.ppermute(values, axis, (pair, pair[::-1]))  5.28 us
    all_to_all x1, waiting for transfers between devices, exchange(): return lax.all_to_all(parts, axis, 0, 0)  5.21 us
  transfers between devices with their start and end apart: 9, of which 7 were waited for; matrix products, arithmetic and copies ran while one was open for 2% of the time, Pallas kernels for 0%

profile of v4, /device:TPU:128, one launch (start us, length us, event | category | flops | bytes accessed | tf_op | source)
XLA Modules:
  0.0 154.4 jit_solution(14012540928782276481)
XLA Ops:
  0.0 1.1 multiply_reduce_fusion
  1.1 0.6 broadcast_in_dim.54
  1.8 8.7 %all-to-all-start = ((f32[32,1,64]{2,1,0:T(1,128)}), f32[32,1,64]{2,1,0:T(1,128)S(1)}, u32[]{:S(2)}, u32[]{:S(2)}) async-start(f32[32,1,64]{2,1,0:T(1,128)} %broadcast_in_dim.54), calls=%async_computation | async-start | bytes 32768 | tf_op jit(solution)/shard_map/all_to_all | solution.py:12
  10.5 0.8 select_reduce_fusion
  11.3 1.3 slice_bitcast_fusion
  12.8 0.1 multiply_sine_fusion
  12.9 5.2 %all-to-all-done = f32[32,1,64]{2,1,0:T(1,128)S(1)} async-done(((f32[32,1,64]{2,1,0:T(1,128)}), f32[32,1,64]{2,1,0:T(1,128)S(1)}, u32[]{:S(2)}, u32[]{:S(2)}) %all-to-all-start) | async-done | bytes 8224 | tf_op jit(solution)/shard_map/all_to_all | solution.py:12
  18.2 0.2 fusion.13
  18.5 0.1 reshape.245
  18.6 12.7 %all_to_all.45 = f32[32,2,768]{2,1,0:T(2,128)S(1)} all-to-all(f32[32,2,768]{2,1,0:T(2,128)S(1)} %reshape.245), channel_id=1, replica_groups=mesh['attn'=32,'ffn'=4,'grp'=4] {'attn'}, dimensions={0} | all-to-all | bytes 393216 | tf_op jit(solution)/shard_map/all_to_all | solution.py:12
  31.6 0.2 multiply_reduce_fusion.2
  31.8 9.6 %all_to_all.46 = bf16[4,2,512]{2,1,0:T(2,128)(2,1)S(1)} all-to-all(bf16[4,2,512]{2,1,0:T(2,128)(2,1)S(1)} %broadcast_in_dim.60), channel_id=1, replica_groups=mesh['attn'=32,'ffn'=4,'grp'=4] {'grp'}, dimensions={0} | all-to-all | bytes 16384 | tf_op jit(solution)/shard_map/all_to_all | solution.py:12
  41.4 0.3 fusion.37
  41.7 0.2 fusion.3
  41.9 0.3 fusion.8
  42.4 7.8 %all_to_all.47 = f32[4,2,4,256]{3,2,1,0:T(4,128)S(1)} all-to-all(f32[4,2,4,256]{3,2,1,0:T(4,128)S(1)} %bitcast.43), channel_id=1, replica_groups=mesh['attn'=32,'ffn'=4,'grp'=4] {'grp'}, dimensions={0} | all-to-all | bytes 65536 | tf_op jit(solution)/shard_map/all_to_all | solution.py:12
  50.2 0.1 slice_reduce_fusion.2
  50.3 0.2 exponential_reduce_fusion
  50.8 11.5 %all_to_all.48 = bf16[32,2,512]{2,1,0:T(2,128)(2,1)S(1)} all-to-all(bf16[32,2,512]{2,1,0:T(2,128)(2,1)S(1)} %broadcast_in_dim.65), channel_id=1, replica_groups=mesh['attn'=32,'ffn'=4,'grp'=4] {'attn'}, dimensions={0} | all-to-all | bytes 131072 | tf_op jit(solution)/shard_map/all_to_all | solution.py:12
  62.3 0.3 fusion.2
  62.7 8.4 %all_to_all.49 = bf16[4,64,256]{2,1,0:T(8,128)(2,1)S(1)} all-to-all(bf16[4,64,256]{2,1,0:T(8,128)(2,1)S(1)} %broadcast_in_dim.66), channel_id=1, replica_groups=mesh['attn'=32,'ffn'=4,'grp'=4] {'grp'}, dimensions={0} | all-to-all | bytes 262144 | tf_op jit(solution)/shard_map/all_to_all | solution.py:12
  71.1 1.9 %collective-permute-start = (bf16[64,256]{1,0:T(8,128)(2,1)S(1)}, bf16[64,256]{1,0:T(8,128)(2,1)S(1)}, u32[]{:S(2)}, u32[]{:S(2)}) collective-permute-start(bf16[64,256]{1,0:T(8,128)(2,1)S(1)} %reduce_sum.122), channel_id=1, source_target_pairs={{0,4},{4,0},{1,5},{5,1},{2,6},{6,2},{3,7},{7,3},{16,20},{20,16},{1... | collective-permute-start | bytes 98312 | tf_op jit(solution)/shard_map/ppermute | solution.py:40
  73.0 7.8 %collective-permute-done = bf16[64,256]{1,0:T(8,128)(2,1)S(1)} collective-permute-done((bf16[64,256]{1,0:T(8,128)(2,1)S(1)}, bf16[64,256]{1,0:T(8,128)(2,1)S(1)}, u32[]{:S(2)}, u32[]{:S(2)}) %collective-permute-start) | collective-permute-done | bytes 32800 | tf_op jit(solution)/shard_map/ppermute | solution.py:40
  80.8 1.3 collective-permute-start.2
  82.1 0.7 collective-permute-start.1
  82.8 1.0 collective-permute-done.2
  83.8 1.3 collective-permute-start.3
  85.1 0.2 copy.35
  85.3 9.1 %collective-permute-done.3 = bf16[64,256]{1,0:T(8,128)(2,1)S(1)} collective-permute-done((bf16[64,256]{1,0:T(8,128)(2,1)S(1)}, bf16[64,256]{1,0:T(8,128)(2,1)S(1)}, u32[]{:S(2)}, u32[]{:S(2)}) %collective-permute-start.3) | collective-permute-done | bytes 32800 | tf_op jit(solution)/shard_map/ppermute | solution.py:43
  94.4 0.1 fusion.6
  94.6 0.4 convolution_convert_fusion
  95.1 0.1 concatenate.31
  95.3 0.2 reshape.252
  95.4 18.0 %all_to_all.50 = bf16[32,2,3456]{2,1,0:T(2,128)(2,1)S(1)} all-to-all(bf16[32,2,3456]{2,1,0:T(2,128)(2,1)S(1)} %reshape.252), channel_id=1, replica_groups=mesh['attn'=32,'ffn'=4,'grp'=4] {'attn'}, dimensions={0} | all-to-all | bytes 884736 | tf_op jit(solution)/shard_map/all_to_all | solution.py:12
  113.4 0.4 convert_reduce_fusion
  113.7 0.2 fusion.30
  114.1 0.1 broadcast_in_dim.69
  114.2 13.4 %all_to_all.51 = bf16[32,2,1664]{2,1,0:T(2,128)(2,1)S(1)} all-to-all(bf16[32,2,1664]{2,1,0:T(2,128)(2,1)S(1)} %broadcast_in_dim.69), channel_id=1, replica_groups=mesh['attn'=32,'ffn'=4,'grp'=4] {'attn'}, dimensions={0} | all-to-all | bytes 425984 | tf_op jit(solution)/shard_map/all_to_all | solution.py:12
  127.7 0.3 convolution_convert_fusion.2
  128.0 8.7 %all_to_all.52 = bf16[4,64,256]{2,1,0:T(8,128)(2,1)S(1)} all-to-all(bf16[4,64,256]{2,1,0:T(8,128)(2,1)S(1)} %broadcast_in_dim.70), channel_id=1, replica_groups=mesh['attn'=32,'ffn'=4,'grp'=4] {'grp'}, dimensions={0} | all-to-all | bytes 262144 | tf_op jit(solution)/shard_map/all_to_all | solution.py:12
  136.8 0.7 collective-permute-start.4
  137.5 1.3 collective-permute-start.6
  138.8 2.0 %collective-permute-start.5 = (bf16[64,256]{1,0:T(8,128)(2,1)S(1)}, bf16[64,256]{1,0:T(8,128)(2,1)S(1)}, u32[]{:S(2)}, u32[]{:S(2)}) collective-permute-start(bf16[64,256]{1,0:T(8,128)(2,1)S(1)} %get-tuple-element.28), channel_id=1, source_target_pairs={{0,4},{4,0},{1,5},{5,1},{2,6},{6,2},{3,7},{7,3},{16,20},{20,16},{1... | collective-permute-start | bytes 98312 | tf_op jit(solution)/shard_map/ppermute | solution.py:40
  140.8 8.1 %collective-permute-done.5 = bf16[64,256]{1,0:T(8,128)(2,1)S(1)} collective-permute-done((bf16[64,256]{1,0:T(8,128)(2,1)S(1)}, bf16[64,256]{1,0:T(8,128)(2,1)S(1)}, u32[]{:S(2)}, u32[]{:S(2)}) %collective-permute-start.5) | collective-permute-done | bytes 32800 | tf_op jit(solution)/shard_map/ppermute | solution.py:40
  149.0 1.7 %collective-permute-done.6 = bf16[80,256]{1,0:T(8,128)(2,1)S(1)} collective-permute-done((bf16[80,256]{1,0:T(8,128)(2,1)S(1)}, bf16[80,256]{1,0:T(8,128)(2,1)S(1)}, u32[]{:S(2)}, u32[]{:S(2)}) %collective-permute-start.6) | collective-permute-done | bytes 40992 | tf_op jit(solution)/shard_map/ppermute | solution.py:43
  150.7 1.5 collective-permute-start.7
  152.2 1.6 %collective-permute-done.7 = bf16[64,256]{1,0:T(8,128)(2,1)S(1)} collective-permute-done((bf16[64,256]{1,0:T(8,128)(2,1)S(1)}, bf16[64,256]{1,0:T(8,128)(2,1)S(1)}, u32[]{:S(2)}, u32[]{:S(2)}) %collective-permute-start.7) | collective-permute-done | bytes 32800 | tf_op jit(solution)/shard_map/ppermute | solution.py:43
  153.8 0.6 fusion.7
  (69 shorter events, 1.7 us)
Async XLA Ops:
  0.0 127.7 %copy-start = (bf16[1664,256]{1,0:T(8,128)(2,1)S(1)}, bf16[1664,256]{1,0:T(8,128)(2,1)}, u32[]{:S(2)}) copy-start(bf16[1664,256]{1,0:T(8,128)(2,1)} %param.18) | copy-start | bytes 2555908
  0.0 12.9 %copy-start.5 = (bf16[256,1,256]{2,0,1:T(8,128)(2,1)S(1)}, bf16[256,1,256]{2,0,1:T(8,128)(2,1)}, u32[]{:S(2)}) copy-start(bf16[256,1,256]{2,0,1:T(8,128)(2,1)} %param.15) | copy-start | bytes 393220
  0.0 12.9 %copy-start.2 = (bf16[256,512]{1,0:T(8,128)(2,1)S(1)}, bf16[256,512]{1,0:T(8,128)(2,1)}, u32[]{:S(2)}) copy-start(bf16[256,512]{1,0:T(8,128)(2,1)} %param.14) | copy-start | bytes 786436
  0.0 18.2 %copy-start.7 = (f32[256]{0:T(256)S(1)}, f32[256]{0:T(256)}, u32[]{:S(2)}) copy-start(f32[256]{0:T(256)} %param.12) | copy-start | bytes 3076
  1.8 16.4 %all-to-all-start = ((f32[32,1,64]{2,1,0:T(1,128)}), f32[32,1,64]{2,1,0:T(1,128)S(1)}, u32[]{:S(2)}, u32[]{:S(2)}) async-start(f32[32,1,64]{2,1,0:T(1,128)} %broadcast_in_dim.54), calls=%async_computation | async-start | bytes 32768 | tf_op jit(solution)/shard_map/all_to_all | solution.py:12
  18.4 43.9 %copy-start.3 = (bf16[512,256]{1,0:T(8,128)(2,1)S(1)}, bf16[512,256]{1,0:T(8,128)(2,1)}, u32[]{:S(2)}) copy-start(bf16[512,256]{1,0:T(8,128)(2,1)} %param.16) | copy-start | bytes 786436
  18.4 43.9 %copy-start.6 = (s32[64]{0:T(128)S(1)}, s32[64]{0:T(128)}, u32[]{:S(2)}) copy-start(s32[64]{0:T(128)} %param.21) | copy-start | bytes 772
  41.7 43.4 %copy-start.1 = (bf16[256,2,1664]{2,1,0:T(2,128)(2,1)S(1)}, bf16[256,2,1664]{2,1,0:T(2,128)(2,1)}, u32[]{:S(2)}) copy-start(bf16[256,2,1664]{2,1,0:T(2,128)(2,1)} %param.17) | copy-start | bytes 5111812
  71.1 9.7 %collective-permute-start = (bf16[64,256]{1,0:T(8,128)(2,1)S(1)}, bf16[64,256]{1,0:T(8,128)(2,1)S(1)}, u32[]{:S(2)}, u32[]{:S(2)}) collective-permute-start(bf16[64,256]{1,0:T(8,128)(2,1)S(1)} %reduce_sum.122), channel_id=1, source_target_pairs={{0,4},{4,0},{1,5},{5,1},{2,6},{6,2},{3,7},{7,3},{16,20},{20,16},{1... | collective-permute-start | bytes 98312 | tf_op jit(solution)/shard_map/ppermute | solution.py:40
  80.8 3.0 %collective-permute-start.2 = (bf16[80,256]{1,0:T(8,128)(2,1)S(1)}, bf16[80,256]{1,0:T(8,128)(2,1)S(1)}, u32[]{:S(2)}, u32[]{:S(2)}) collective-permute-start(bf16[80,256]{1,0:T(8,128)(2,1)S(1)} %pad.7), channel_id=1, source_target_pairs={{0,12},{4,8},{1,13},{5,9},{2,14},{6,10},{3,15},{7,11},{16,28},{20,... | collective-permute-start | bytes 122888 | tf_op jit(solution)/shard_map/ppermute | solution.py:43
  82.1 0.7 collective-permute-start.1
  83.8 10.6 %collective-permute-start.3 = (bf16[64,256]{1,0:T(8,128)(2,1)S(1)}, bf16[64,256]{1,0:T(8,128)(2,1)S(1)}, u32[]{:S(2)}, u32[]{:S(2)}) collective-permute-start(bf16[64,256]{1,0:T(8,128)(2,1)S(1)} %broadcast_select_fusion.2), channel_id=1, source_target_pairs={{12,0},{8,4},{13,1},{9,5},{14,2},{10,6},{15,3},{11,7},{28,16},{24,... | collective-permute-start | bytes 98312 | tf_op jit(solution)/shard_map/ppermute | solution.py:43
  85.1 9.3 %copy-start.4 = (bf16[64,256]{1,0:T(8,128)(2,1)S(1)}, bf16[64,256]{1,0:T(8,128)(2,1)}, u32[]{:S(2)}) copy-start(bf16[64,256]{1,0:T(8,128)(2,1)} %param.11) | copy-start | bytes 98308
  85.1 9.5 %copy-start.8 = (f32[256]{0:T(256)S(1)}, f32[256]{0:T(256)}, u32[]{:S(2)}) copy-start(f32[256]{0:T(256)} %param.13) | copy-start | bytes 3076
  136.8 0.7 collective-permute-start.4
  137.5 13.2 %collective-permute-start.6 = (bf16[80,256]{1,0:T(8,128)(2,1)S(1)}, bf16[80,256]{1,0:T(8,128)(2,1)S(1)}, u32[]{:S(2)}, u32[]{:S(2)}) collective-permute-start(bf16[80,256]{1,0:T(8,128)(2,1)S(1)} %pad.8), channel_id=1, source_target_pairs={{12,0},{8,4},{13,1},{9,5},{14,2},{10,6},{15,3},{11,7},{28,16},{24,... | collective-permute-start | bytes 122888 | tf_op jit(solution)/shard_map/ppermute | solution.py:43
  138.8 10.2 %collective-permute-start.5 = (bf16[64,256]{1,0:T(8,128)(2,1)S(1)}, bf16[64,256]{1,0:T(8,128)(2,1)S(1)}, u32[]{:S(2)}, u32[]{:S(2)}) collective-permute-start(bf16[64,256]{1,0:T(8,128)(2,1)S(1)} %get-tuple-element.28), channel_id=1, source_target_pairs={{0,4},{4,0},{1,5},{5,1},{2,6},{6,2},{3,7},{7,3},{16,20},{20,16},{1... | collective-permute-start | bytes 98312 | tf_op jit(solution)/shard_map/ppermute | solution.py:40
  150.7 3.1 %collective-permute-start.7 = (bf16[64,256]{1,0:T(8,128)(2,1)S(1)}, bf16[64,256]{1,0:T(8,128)(2,1)S(1)}, u32[]{:S(2)}, u32[]{:S(2)}) collective-permute-start(bf16[64,256]{1,0:T(8,128)(2,1)S(1)} %broadcast_select_fusion), channel_id=1, source_target_pairs={{0,12},{4,8},{1,13},{5,9},{2,14},{6,10},{3,15},{7,11},{16,28},{20,... | collective-permute-start | bytes 98312 | tf_op jit(solution)/shard_map/ppermute | solution.py:43

commit v5 on v4

--- a/solution.py
+++ b/solution.py
@@ -1,6 +1,7 @@
 import jax
 import jax.numpy as jnp
 from jax import lax
+from jax.sharding import Mesh
 from jax.sharding import PartitionSpec as P
 
 D = 8192
@@ -8,12 +9,15 @@
 BF16 = jnp.bfloat16
 
 
+ATTN = ("chip", "core")
+
+
 def exchange(parts, axis):
     return lax.all_to_all(parts, axis, 0, 0)
 
 
 def spread(part, axis):
-    count = lax.axis_size(axis)
+    count = lax.psum(1, axis)
     return exchange(jnp.broadcast_to(part[None], (count,) + part.shape), axis)
 
 
@@ -82,7 +86,7 @@
     head_size = cache.shape[3] // 2
     query_cols = w_query.shape[1]
     heads_mine = query_cols // head_size
-    attn_count = lax.axis_size("attn")
+    attn_count = lax.psum(1, ATTN)
     grp_count = lax.axis_size("grp")
     heads_all = heads_mine * grp_count
     scale = head_size ** (-0.5)
@@ -90,11 +94,11 @@
     matches = request_slot[None, :] == order[:, None]
     slot_rows = dot(matches.astype(BF16), layer_in)
     squares = jnp.sum(slot_rows * slot_rows, axis=1)
-    squares = spread(squares[None], "attn")
+    squares = spread(squares[None], ATTN)
 
     slot_length = jnp.sum(jnp.where(matches, cache_len[None, :], 0), axis=1)
     my_length = lax.dynamic_slice_in_dim(
-        slot_length, lax.axis_index("attn") * req_here, req_here, 0
+        slot_length, lax.axis_index(ATTN) * req_here, req_here, 0
     )
     cosine, sine = angles(my_length.astype(F32), head_size)
     positions = lax.axis_index("grp") * slots_here + jnp.arange(slots_here, dtype=jnp.int32)
@@ -108,7 +112,7 @@
     squares = jnp.sum(squares, (0, 1))
     normed = (slot_rows * lax.rsqrt(squares / D + 1e-05)[:, None] * gain_attn).astype(BF16)
     packed = dot(normed, weights)
-    summed = exchange(packed.reshape(attn_count, req_here, -1), "attn")
+    summed = exchange(packed.reshape(attn_count, req_here, -1), ATTN)
     summed = jnp.sum(summed, 0)
     queries = rotate(
         summed[:, :query_cols].reshape(req_here, heads_mine, head_size), cosine, sine
@@ -150,7 +154,7 @@
     attended = jnp.sum(mixed * factor[..., None], 0)
     attended = attended + own_weight[..., None] * new_value[:, None, :]
     attended = (attended / denom[..., None]).astype(BF16).reshape(req_here, query_cols)
-    attended = spread(attended, "attn").reshape(requests, query_cols)
+    attended = spread(attended, ATTN).reshape(requests, query_cols)
     to_requests = (request_slot[:, None] == order[None, :]).astype(BF16)
     attended = dot(to_requests, attended).astype(BF16)
     resid = layer_in.astype(F32)
@@ -161,41 +165,43 @@
     squares = jnp.sum(middle_float * middle_float, axis=1)
     squares_high = squares.astype(BF16)
     squares_low = (squares - squares_high.astype(F32)).astype(BF16)
-    half = (requests, 64)
     units = w_gate_up.shape[2]
     both = dot((middle_float * gain_ffn).astype(BF16), w_gate_up.reshape(w_gate_up.shape[0], -1))
-    packed = jnp.concatenate(
-        [
-            both.astype(BF16),
-            jnp.broadcast_to(squares_high[:, None], half),
-            jnp.broadcast_to(squares_low[:, None], half),
-        ],
-        1,
-    )
-    packed = exchange(packed.reshape(attn_count, req_here, -1), "attn").astype(F32)
+    core = lax.axis_index("core")
+    lane = jnp.arange(128, dtype=jnp.int32)[None, :]
+    tail = jnp.where(lane % 64 < 32, squares_high[:, None], squares_low[:, None])
+    tail = jnp.where(lane // 64 == core, tail, jnp.zeros((), BF16))
+    packed = jnp.concatenate([both.astype(BF16), tail], 1)
+    packed = packed.reshape(attn_count // 2, 2, req_here, -1)
+    kept = lax.dynamic_index_in_dim(packed, core, 1, False)
+    given = lax.dynamic_index_in_dim(packed, 1 - core, 1, False)
+    pair = kept.astype(F32) + lax.ppermute(given, "core", ((0, 1), (1, 0))).astype(F32)
+    packed = exchange(pair.astype(BF16), "chip").astype(F32)
     summed = jnp.sum(packed, 0)
-    squares = summed[:, 2 * units] + summed[:, 2 * units + 64]
+    squares = sum(summed[:, 2 * units + start] for start in (0, 32, 64, 96))
     summed = summed * lax.rsqrt(squares / D + 1e-05)[:, None]
     active = (jax.nn.silu(summed[:, :units]) * summed[:, units : 2 * units]).astype(BF16)
-    active = spread(active, "attn").reshape(requests, units)
+    active = spread(active, ATTN).reshape(requests, units)
     down = sum_spread(dot(active, w_down), "grp")
     return (middle_float + sum_relay(down, "ffn", (3, 2), (0, 1))).astype(BF16)
 
 
 def solution(mesh):
+    attn, ffn, grp = mesh.devices.shape
+    cut = Mesh(mesh.devices.reshape(attn // 2, 2, ffn, grp), ATTN + ("ffn", "grp"))
     placed = (
-        P(None, "attn"),
-        P("attn"),
-        P("attn"),
-        P("attn", ("ffn", "grp")),
-        P("attn", "ffn", None),
-        P(("ffn", "grp"), "attn"),
-        P("attn", None, ("ffn", "grp")),
-        P(("ffn", "grp"), "attn"),
-        P("attn", "ffn", "grp", None),
+        P(None, ATTN),
+        P(ATTN),
+        P(ATTN),
+        P(ATTN, ("ffn", "grp")),
+        P(ATTN, "ffn", None),
+        P(("ffn", "grp"), ATTN),
+        P(ATTN, None, ("ffn", "grp")),
+        P(("ffn", "grp"), ATTN),
+        P(ATTN, "ffn", "grp", None),
         P(),
         P(),
     )
     return jax.shard_map(
-        shards, mesh=mesh, in_specs=placed, out_specs=P(None, "attn"), check_vma=False
-    )
+        shards, mesh=cut, in_specs=placed, out_specs=P(None, ATTN), check_vma=False
+    )

time: 155 us -> 153 us (0.987)
  blocking collectives: 90 us -> 84.9 us
  starting transfers between devices: 19.4 us -> 21.3 us
    all_to_all x8, blocking collectives: 90 us -> 84.9 us  [exchange(): return lax.all_to_all(parts, axis, 0, 0)]
    ppermute x0 -> x1, starting transfers between devices: none -> 1.92 us  [shards(): lax.ppermute(given, 'core', ((0, 1), (1, 0))).astype(F32)]
  transfers between devices with their start and end apart: 9 -> 10, of which waited for: 7 -> 8; matrix products, arithmetic and copies ran while one was open for 2% -> 3% of each run, Pallas kernels for 0% -> 0%
where the time goes in v5:
time: 153 us
  blocking collectives  84.9 us (55%)
  waiting for transfers between devices  34.5 us (23%)
  starting transfers between devices  21.3 us (14%)
  local copies, waits for them, and re-layouts  4.57 us (3%)
  other arithmetic  4.09 us (3%)
  matrix products  2.92 us (2%)
    all_to_all x8, blocking collectives, exchange(): return lax.all_to_all(parts, axis, 0, 0)  84.9 us
    ppermute x4, waiting for transfers between devices, swap(): return lax.ppermute(values, axis, (pair, pair[::-1]))  16 us
    ppermute x4, waiting for transfers between devices, hand(): return lax.ppermute(values, axis, tuple(zip(sources, targets)))  11.8 us
    all_to_all x1, starting transfers between devices, exchange(): return lax.all_to_all(parts, axis, 0, 0)  8.75 us
    ppermute x4, starting transfers between devices, hand(): return lax.ppermute(values, axis, tuple(zip(sources, targets)))  5.36 us
    ppermute x4, starting transfers between devices, swap(): return lax.ppermute(values, axis, (pair, pair[::-1]))  5.28 us
    all_to_all x1, waiting for transfers between devices, exchange(): return lax.all_to_all(parts, axis, 0, 0)  5.2 us
  transfers between devices with their start and end apart: 10, of which 8 were waited for; matrix products, arithmetic and copies ran while one was open for 3% of the time, Pallas kernels for 0%

profile of v5, /device:TPU:128, one launch (start us, length us, event | category | flops | bytes accessed | tf_op | source)
XLA Modules:
  0.0 152.7 jit_solution(4978645200054579269)
XLA Ops:
  0.0 1.1 multiply_reduce_fusion
  1.1 0.6 broadcast_in_dim.82
  1.8 8.7 %all-to-all-start = ((f32[32,1,64]{2,1,0:T(1,128)}), f32[32,1,64]{2,1,0:T(1,128)S(1)}, u32[]{:S(2)}, u32[]{:S(2)}) async-start(f32[32,1,64]{2,1,0:T(1,128)} %broadcast_in_dim.82), calls=%async_computation | async-start | bytes 32768 | tf_op jit(solution)/shard_map/all_to_all | solution.py:16
  10.5 0.8 select_reduce_fusion
  11.3 1.3 slice_bitcast_fusion
  12.9 5.2 %all-to-all-done = f32[32,1,64]{2,1,0:T(1,128)S(1)} async-done(((f32[32,1,64]{2,1,0:T(1,128)}), f32[32,1,64]{2,1,0:T(1,128)S(1)}, u32[]{:S(2)}, u32[]{:S(2)}) %all-to-all-start) | async-done | bytes 8224 | tf_op jit(solution)/shard_map/all_to_all | solution.py:16
  18.2 0.2 fusion.14
  18.6 12.7 %all_to_all.45 = f32[32,2,768]{2,1,0:T(2,128)S(1)} all-to-all(f32[32,2,768]{2,1,0:T(2,128)S(1)} %reshape.303), channel_id=1, replica_groups=mesh['chip'=16,'core'=2,'ffn'=4,'grp'=4] {'chip','core'}, dimensions={0} | all-to-all | bytes 393216 | tf_op jit(solution)/shard_map/all_to_all | solution.py:16
  31.6 0.2 multiply_reduce_fusion.2
  31.8 9.6 %all_to_all.46 = bf16[4,2,512]{2,1,0:T(2,128)(2,1)S(1)} all-to-all(bf16[4,2,512]{2,1,0:T(2,128)(2,1)S(1)} %broadcast_in_dim.92), channel_id=1, replica_groups=mesh['chip'=16,'core'=2,'ffn'=4,'grp'=4] {'grp'}, dimensions={0} | all-to-all | bytes 16384 | tf_op jit(solution)/shard_map/all_to_all | solution.py:16
  41.4 0.3 fusion.41
  41.7 0.2 fusion.4
  41.9 0.3 fusion.9
  42.4 7.8 %all_to_all.47 = f32[4,2,4,256]{3,2,1,0:T(4,128)S(1)} all-to-all(f32[4,2,4,256]{3,2,1,0:T(4,128)S(1)} %bitcast.50), channel_id=1, replica_groups=mesh['chip'=16,'core'=2,'ffn'=4,'grp'=4] {'grp'}, dimensions={0} | all-to-all | bytes 65536 | tf_op jit(solution)/shard_map/all_to_all | solution.py:16
  50.3 0.2 exponential_reduce_fusion
  50.8 11.5 %all_to_all.48 = bf16[32,2,512]{2,1,0:T(2,128)(2,1)S(1)} all-to-all(bf16[32,2,512]{2,1,0:T(2,128)(2,1)S(1)} %broadcast_in_dim.97), channel_id=1, replica_groups=mesh['chip'=16,'core'=2,'ffn'=4,'grp'=4] {'chip','core'}, dimensions={0} | all-to-all | bytes 131072 | tf_op jit(solution)/shard_map/all_to_all | solution.py:16
  62.3 0.3 fusion.2
  62.7 8.4 %all_to_all.49 = bf16[4,64,256]{2,1,0:T(8,128)(2,1)S(1)} all-to-all(bf16[4,64,256]{2,1,0:T(8,128)(2,1)S(1)} %broadcast_in_dim.154), channel_id=1, replica_groups=mesh['chip'=16,'core'=2,'ffn'=4,'grp'=4] {'grp'}, dimensions={0} | all-to-all | bytes 262144 | tf_op jit(solution)/shard_map/all_to_all | solution.py:16
  71.1 1.9 %collective-permute-start = (bf16[64,256]{1,0:T(8,128)(2,1)S(1)}, bf16[64,256]{1,0:T(8,128)(2,1)S(1)}, u32[]{:S(2)}, u32[]{:S(2)}) collective-permute-start(bf16[64,256]{1,0:T(8,128)(2,1)S(1)} %reduce_sum.122), channel_id=1, source_target_pairs={{0,4},{4,0},{1,5},{5,1},{2,6},{6,2},{3,7},{7,3},{16,20},{20,16},{1... | collective-permute-start | bytes 98312 | tf_op jit(solution)/shard_map/ppermute | solution.py:44
  73.0 7.8 %collective-permute-done = bf16[64,256]{1,0:T(8,128)(2,1)S(1)} collective-permute-done((bf16[64,256]{1,0:T(8,128)(2,1)S(1)}, bf16[64,256]{1,0:T(8,128)(2,1)S(1)}, u32[]{:S(2)}, u32[]{:S(2)}) %collective-permute-start) | collective-permute-done | bytes 32800 | tf_op jit(solution)/shard_map/ppermute | solution.py:44
  80.8 1.3 collective-permute-start.2
  82.1 0.7 collective-permute-start.1
  82.8 1.0 collective-permute-done.2
  83.8 1.3 collective-permute-start.3
  85.1 1.6 %copy.40 = bf16[32,8,2,1664]{3,1,2,0:T(8,128)(2,1)S(1)} copy(bf16[32,8,2,1664]{3,2,1,0:T(2,128)(2,1)} %bitcast.49) | data formatting | bytes 3407872
  86.8 7.6 %collective-permute-done.3 = bf16[64,256]{1,0:T(8,128)(2,1)S(1)} collective-permute-done((bf16[64,256]{1,0:T(8,128)(2,1)S(1)}, bf16[64,256]{1,0:T(8,128)(2,1)S(1)}, u32[]{:S(2)}, u32[]{:S(2)}) %collective-permute-start.3) | collective-permute-done | bytes 32800 | tf_op jit(solution)/shard_map/ppermute | solution.py:47
  94.4 0.1 fusion.7
  94.6 0.4 convolution_convert_fusion
  95.1 0.2 reshape.310
  95.3 0.2 dynamic-slice_bitcast_fusion
  95.5 1.9 %collective-permute-start.4 = (bf16[16,2,3456]{2,1,0:T(2,128)(2,1)S(1)}, bf16[16,2,3456]{2,1,0:T(2,128)(2,1)S(1)}, u32[]{:S(2)}, u32[]{:S(2)}) collective-permute-start(bf16[16,2,3456]{2,1,0:T(2,128)(2,1)S(1)} %dynamic-slice_bitcast_fusion), channel_id=1, source_target_pairs={{0,16},{16,0},{1,17},{17,1},{2,18},{18,2},{3,19},{19,3},{4,20},{20... | collective-permute-start | bytes 663560 | tf_op jit(solution)/shard_map/ppermute | solution.py:178
  97.4 1.4 collective-permute-done.4
  98.8 0.2 fusion.3
  99.1 13.2 %all_to_all.50 = bf16[16,2,3456]{2,1,0:T(2,128)(2,1)S(1)} all-to-all(bf16[16,2,3456]{2,1,0:T(2,128)(2,1)S(1)} %fusion.3), channel_id=1, replica_groups=mesh['chip'=16,'core'=2,'ffn'=4,'grp'=4] {'chip'}, dimensions={0} | all-to-all | bytes 442368 | tf_op jit(solution)/shard_map/all_to_all | solution.py:16
  112.3 0.2 convert_reduce_fusion
  112.4 0.2 fusion.31
  112.8 0.1 broadcast_in_dim.160
  112.9 13.1 %all_to_all.51 = bf16[32,2,1664]{2,1,0:T(2,128)(2,1)S(1)} all-to-all(bf16[32,2,1664]{2,1,0:T(2,128)(2,1)S(1)} %broadcast_in_dim.160), channel_id=1, replica_groups=mesh['chip'=16,'core'=2,'ffn'=4,'grp'=4] {'chip','core'}, dimensions={0} | all-to-all | bytes 425984 | tf_op jit(solution)/shard_map/all_to_all | solution.py:16
  126.0 0.3 convolution_convert_fusion.2
  126.3 8.7 %all_to_all.52 = bf16[4,64,256]{2,1,0:T(8,128)(2,1)S(1)} all-to-all(bf16[4,64,256]{2,1,0:T(8,128)(2,1)S(1)} %broadcast_in_dim.161), channel_id=1, replica_groups=mesh['chip'=16,'core'=2,'ffn'=4,'grp'=4] {'grp'}, dimensions={0} | all-to-all | bytes 262144 | tf_op jit(solution)/shard_map/all_to_all | solution.py:16
  135.1 0.7 collective-permute-start.5
  135.8 1.3 collective-permute-start.7
  137.1 2.0 %collective-permute-start.6 = (bf16[64,256]{1,0:T(8,128)(2,1)S(1)}, bf16[64,256]{1,0:T(8,128)(2,1)S(1)}, u32[]{:S(2)}, u32[]{:S(2)}) collective-permute-start(bf16[64,256]{1,0:T(8,128)(2,1)S(1)} %get-tuple-element.28), channel_id=1, source_target_pairs={{0,4},{4,0},{1,5},{5,1},{2,6},{6,2},{3,7},{7,3},{16,20},{20,16},{1... | collective-permute-start | bytes 98312 | tf_op jit(solution)/shard_map/ppermute | solution.py:44
  139.2 8.2 %collective-permute-done.6 = bf16[64,256]{1,0:T(8,128)(2,1)S(1)} collective-permute-done((bf16[64,256]{1,0:T(8,128)(2,1)S(1)}, bf16[64,256]{1,0:T(8,128)(2,1)S(1)}, u32[]{:S(2)}, u32[]{:S(2)}) %collective-permute-start.6) | collective-permute-done | bytes 32800 | tf_op jit(solution)/shard_map/ppermute | solution.py:44
  147.4 1.6 %collective-permute-done.7 = bf16[80,256]{1,0:T(8,128)(2,1)S(1)} collective-permute-done((bf16[80,256]{1,0:T(8,128)(2,1)S(1)}, bf16[80,256]{1,0:T(8,128)(2,1)S(1)}, u32[]{:S(2)}, u32[]{:S(2)}) %collective-permute-start.7) | collective-permute-done | bytes 40992 | tf_op jit(solution)/shard_map/ppermute | solution.py:47
  149.0 1.5 collective-permute-start.8
  150.5 1.6 %collective-permute-done.8 = bf16[64,256]{1,0:T(8,128)(2,1)S(1)} collective-permute-done((bf16[64,256]{1,0:T(8,128)(2,1)S(1)}, bf16[64,256]{1,0:T(8,128)(2,1)S(1)}, u32[]{:S(2)}, u32[]{:S(2)}) %collective-permute-start.8) | collective-permute-done | bytes 32800 | tf_op jit(solution)/shard_map/ppermute | solution.py:47
  152.1 0.6 fusion.8
  (71 shorter events, 2.0 us)
Async XLA Ops:
  0.0 126.0 %copy-start = (bf16[1664,256]{1,0:T(8,128)(2,1)S(1)}, bf16[1664,256]{1,0:T(8,128)(2,1)}, u32[]{:S(2)}) copy-start(bf16[1664,256]{1,0:T(8,128)(2,1)} %param.18) | copy-start | bytes 2555908
  0.0 12.9 %copy-start.4 = (bf16[256,1,256]{2,0,1:T(8,128)(2,1)S(1)}, bf16[256,1,256]{2,0,1:T(8,128)(2,1)}, u32[]{:S(2)}) copy-start(bf16[256,1,256]{2,0,1:T(8,128)(2,1)} %param.15) | copy-start | bytes 393220
  0.0 12.9 %copy-start.1 = (bf16[256,512]{1,0:T(8,128)(2,1)S(1)}, bf16[256,512]{1,0:T(8,128)(2,1)}, u32[]{:S(2)}) copy-start(bf16[256,512]{1,0:T(8,128)(2,1)} %param.14) | copy-start | bytes 786436
  0.0 18.2 %copy-start.6 = (f32[256]{0:T(256)S(1)}, f32[256]{0:T(256)}, u32[]{:S(2)}) copy-start(f32[256]{0:T(256)} %param.12) | copy-start | bytes 3076
  1.8 16.4 %all-to-all-start = ((f32[32,1,64]{2,1,0:T(1,128)}), f32[32,1,64]{2,1,0:T(1,128)S(1)}, u32[]{:S(2)}, u32[]{:S(2)}) async-start(f32[32,1,64]{2,1,0:T(1,128)} %broadcast_in_dim.82), calls=%async_computation | async-start | bytes 32768 | tf_op jit(solution)/shard_map/all_to_all | solution.py:16
  18.4 43.9 %copy-start.2 = (bf16[512,256]{1,0:T(8,128)(2,1)S(1)}, bf16[512,256]{1,0:T(8,128)(2,1)}, u32[]{:S(2)}) copy-start(bf16[512,256]{1,0:T(8,128)(2,1)} %param.16) | copy-start | bytes 786436
  18.4 43.9 %copy-start.5 = (s32[64]{0:T(128)S(1)}, s32[64]{0:T(128)}, u32[]{:S(2)}) copy-start(s32[64]{0:T(128)} %param.21) | copy-start | bytes 772
  71.1 9.7 %collective-permute-start = (bf16[64,256]{1,0:T(8,128)(2,1)S(1)}, bf16[64,256]{1,0:T(8,128)(2,1)S(1)}, u32[]{:S(2)}, u32[]{:S(2)}) collective-permute-start(bf16[64,256]{1,0:T(8,128)(2,1)S(1)} %reduce_sum.122), channel_id=1, source_target_pairs={{0,4},{4,0},{1,5},{5,1},{2,6},{6,2},{3,7},{7,3},{16,20},{20,16},{1... | collective-permute-start | bytes 98312 | tf_op jit(solution)/shard_map/ppermute | solution.py:44
  80.8 3.0 %collective-permute-start.2 = (bf16[80,256]{1,0:T(8,128)(2,1)S(1)}, bf16[80,256]{1,0:T(8,128)(2,1)S(1)}, u32[]{:S(2)}, u32[]{:S(2)}) collective-permute-start(bf16[80,256]{1,0:T(8,128)(2,1)S(1)} %pad.7), channel_id=1, source_target_pairs={{0,12},{4,8},{1,13},{5,9},{2,14},{6,10},{3,15},{7,11},{16,28},{20,... | collective-permute-start | bytes 122888 | tf_op jit(solution)/shard_map/ppermute | solution.py:47
  82.1 0.7 collective-permute-start.1
  83.8 10.6 %collective-permute-start.3 = (bf16[64,256]{1,0:T(8,128)(2,1)S(1)}, bf16[64,256]{1,0:T(8,128)(2,1)S(1)}, u32[]{:S(2)}, u32[]{:S(2)}) collective-permute-start(bf16[64,256]{1,0:T(8,128)(2,1)S(1)} %broadcast_select_fusion.2), channel_id=1, source_target_pairs={{12,0},{8,4},{13,1},{9,5},{14,2},{10,6},{15,3},{11,7},{28,16},{24,... | collective-permute-start | bytes 98312 | tf_op jit(solution)/shard_map/ppermute | solution.py:47
  85.1 9.3 %copy-start.3 = (bf16[64,256]{1,0:T(8,128)(2,1)S(1)}, bf16[64,256]{1,0:T(8,128)(2,1)}, u32[]{:S(2)}) copy-start(bf16[64,256]{1,0:T(8,128)(2,1)} %param.11) | copy-start | bytes 98308
  85.1 9.5 %copy-start.7 = (f32[256]{0:T(256)S(1)}, f32[256]{0:T(256)}, u32[]{:S(2)}) copy-start(f32[256]{0:T(256)} %param.13) | copy-start | bytes 3076
  95.5 3.4 %collective-permute-start.4 = (bf16[16,2,3456]{2,1,0:T(2,128)(2,1)S(1)}, bf16[16,2,3456]{2,1,0:T(2,128)(2,1)S(1)}, u32[]{:S(2)}, u32[]{:S(2)}) collective-permute-start(bf16[16,2,3456]{2,1,0:T(2,128)(2,1)S(1)} %dynamic-slice_bitcast_fusion), channel_id=1, source_target_pairs={{0,16},{16,0},{1,17},{17,1},{2,18},{18,2},{3,19},{19,3},{4,20},{20... | collective-permute-start | bytes 663560 | tf_op jit(solution)/shard_map/ppermute | solution.py:178
  135.1 0.7 collective-permute-start.5
  135.8 13.2 %collective-permute-start.7 = (bf16[80,256]{1,0:T(8,128)(2,1)S(1)}, bf16[80,256]{1,0:T(8,128)(2,1)S(1)}, u32[]{:S(2)}, u32[]{:S(2)}) collective-permute-start(bf16[80,256]{1,0:T(8,128)(2,1)S(1)} %pad.8), channel_id=1, source_target_pairs={{12,0},{8,4},{13,1},{9,5},{14,2},{10,6},{15,3},{11,7},{28,16},{24,... | collective-permute-start | bytes 122888 | tf_op jit(solution)/shard_map/ppermute | solution.py:47
  137.1 10.3 %collective-permute-start.6 = (bf16[64,256]{1,0:T(8,128)(2,1)S(1)}, bf16[64,256]{1,0:T(8,128)(2,1)S(1)}, u32[]{:S(2)}, u32[]{:S(2)}) collective-permute-start(bf16[64,256]{1,0:T(8,128)(2,1)S(1)} %get-tuple-element.28), channel_id=1, source_target_pairs={{0,4},{4,0},{1,5},{5,1},{2,6},{6,2},{3,7},{7,3},{16,20},{20,16},{1... | collective-permute-start | bytes 98312 | tf_op jit(solution)/shard_map/ppermute | solution.py:44
  149.0 3.1 %collective-permute-start.8 = (bf16[64,256]{1,0:T(8,128)(2,1)S(1)}, bf16[64,256]{1,0:T(8,128)(2,1)S(1)}, u32[]{:S(2)}, u32[]{:S(2)}) collective-permute-start(bf16[64,256]{1,0:T(8,128)(2,1)S(1)} %broadcast_select_fusion), channel_id=1, source_target_pairs={{0,12},{4,8},{1,13},{5,9},{2,14},{6,10},{3,15},{7,11},{16,28},{20,... | collective-permute-start | bytes 98312 | tf_op jit(solution)/shard_map/ppermute | solution.py:47

commit v6 on v5

--- a/solution.py
+++ b/solution.py
@@ -39,7 +39,7 @@
     return jnp.dot(a, b, preferred_element_type=F32)
 
 
-def sum_relay(part, axis, ahead, behind):
+def sum_relay(part, axis, ahead, behind, tied):
     def swap(values, pair):
         return lax.ppermute(values, axis, (pair, pair[::-1]))
 
@@ -50,14 +50,15 @@
         return (one.astype(F32) + two.astype(F32)).astype(BF16)
 
     mine = part.astype(BF16)
-    from_ahead = swap(mine, ahead)
+    here = (lax.axis_index(axis) == ahead[0]) | (lax.axis_index(axis) == ahead[1])
+    from_ahead = lax.cond(here, lambda values: swap(values, ahead), jnp.zeros_like, mine)
     sum_ahead = add(mine, from_ahead)
-    here = (lax.axis_index(axis) == ahead[0]) | (lax.axis_index(axis) == ahead[1])
     down = hand(jnp.pad(sum_ahead, ((0, 16), (0, 0))), ahead, behind)[: part.shape[0]]
     mine = jnp.where(here, sum_ahead, mine)
-    from_behind = swap(mine, behind)
+    from_behind = lax.cond(here, jnp.zeros_like, lambda values: swap(values, behind), mine)
     sum_behind = add(mine, from_behind)
-    up = hand(jnp.where(here, down, sum_behind), behind, ahead)
+    sent = jnp.where(here, down, sum_behind) if tied else sum_behind
+    up = hand(sent, behind, ahead)
     near = jnp.where(here, sum_ahead, sum_behind)
     far = jnp.where(here, up, down)
     return near.astype(F32) + far.astype(F32)
@@ -159,7 +160,7 @@
     attended = dot(to_requests, attended).astype(BF16)
     resid = layer_in.astype(F32)
     projected = sum_spread(dot(attended, w_out), "grp")
-    middle = (resid + sum_relay(projected, "ffn", (0, 1), (3, 2))).astype(BF16)
+    middle = (resid + sum_relay(projected, "ffn", (0, 1), (3, 2), True)).astype(BF16)
 
     middle_float = middle.astype(F32)
     squares = jnp.sum(middle_float * middle_float, axis=1)
@@ -183,7 +184,7 @@
     active = (jax.nn.silu(summed[:, :units]) * summed[:, units : 2 * units]).astype(BF16)
     active = spread(active, ATTN).reshape(requests, units)
     down = sum_spread(dot(active, w_down), "grp")
-    return (middle_float + sum_relay(down, "ffn", (3, 2), (0, 1))).astype(BF16)
+    return (middle_float + sum_relay(down, "ffn", (3, 2), (0, 1), False)).astype(BF16)
 
 
 def solution(mesh):

time: 153 us -> 156 us (1.020)
  the two profiles are of different devices: /device:TPU:128 before, /device:TPU:2 now
where the time goes in v6:
time: 156 us; the launch traced here: 155 us
  blocking collectives  67.3 us (43%)
  starting transfers between devices  40 us (26%)
  waiting for transfers between devices  34 us (22%)
  local copies, waits for them, and re-layouts  5.86 us (4%)
  other arithmetic  4.08 us (3%)
  matrix products  2.92 us (2%)
    all_to_all x6, blocking collectives, exchange(): return lax.all_to_all(parts, axis, 0, 0)  67.3 us
    ppermute x2, starting transfers between devices, swap(): return lax.ppermute(values, axis, (pair, pair[::-1]))  16.8 us
    all_to_all x3, waiting for transfers between devices, exchange(): return lax.all_to_all(parts, axis, 0, 0)  16.3 us
    all_to_all x3, starting transfers between devices, exchange(): return lax.all_to_all(parts, axis, 0, 0)  16.1 us
    ppermute x4, waiting for transfers between devices, hand(): return lax.ppermute(values, axis, tuple(zip(sources, targets)))  10.4 us
    ppermute x2, waiting for transfers between devices, swap(): return lax.ppermute(values, axis, (pair, pair[::-1]))  5.86 us
    ppermute x4, starting transfers between devices, hand(): return lax.ppermute(values, axis, tuple(zip(sources, targets)))  5.17 us
  transfers between devices with their start and end apart: 10, of which 9 were waited for; matrix products, arithmetic and copies ran while one was open for 3% of the time, Pallas kernels for 0%

profile of v6, /device:TPU:2, one launch (start us, length us, event | category | flops | bytes accessed | tf_op | source)
XLA Modules:
  0.0 154.7 jit_solution(2325640745161582710)
XLA Ops:
  0.0 1.1 multiply_reduce_fusion
  1.1 0.6 broadcast_in_dim.82
  1.8 9.4 %all-to-all-start = ((f32[32,1,64]{2,1,0:T(1,128)}), f32[32,1,64]{2,1,0:T(1,128)S(1)}, u32[]{:S(2)}, u32[]{:S(2)}) async-start(f32[32,1,64]{2,1,0:T(1,128)} %broadcast_in_dim.82), calls=%async_computation | async-start | bytes 32768 | tf_op jit(solution)/shard_map/all_to_all | solution.py:16
  11.2 0.8 select_reduce_fusion
  12.0 1.3 slice_bitcast_fusion
  13.6 4.1 %all-to-all-done = f32[32,1,64]{2,1,0:T(1,128)S(1)} async-done(((f32[32,1,64]{2,1,0:T(1,128)}), f32[32,1,64]{2,1,0:T(1,128)S(1)}, u32[]{:S(2)}, u32[]{:S(2)}) %all-to-all-start) | async-done | bytes 8224 | tf_op jit(solution)/shard_map/all_to_all | solution.py:16
  17.8 0.2 fusion.14
  18.1 12.7 %all_to_all.45 = f32[32,2,768]{2,1,0:T(2,128)S(1)} all-to-all(f32[32,2,768]{2,1,0:T(2,128)S(1)} %reshape.303), channel_id=1, replica_groups=mesh['chip'=16,'core'=2,'ffn'=4,'grp'=4] {'chip','core'}, dimensions={0} | all-to-all | bytes 393216 | tf_op jit(solution)/shard_map/all_to_all | solution.py:16
  31.4 9.1 %all_to_all.46 = bf16[4,2,512]{2,1,0:T(2,128)(2,1)S(1)} all-to-all(bf16[4,2,512]{2,1,0:T(2,128)(2,1)S(1)} %broadcast_in_dim.92), channel_id=1, replica_groups=mesh['chip'=16,'core'=2,'ffn'=4,'grp'=4] {'grp'}, dimensions={0} | all-to-all | bytes 16384 | tf_op jit(solution)/shard_map/all_to_all | solution.py:16
  40.5 0.3 fusion.41
  40.9 0.2 fusion.4
  41.0 0.3 fusion.9
  41.6 7.8 %all_to_all.47 = f32[4,2,4,256]{3,2,1,0:T(4,128)S(1)} all-to-all(f32[4,2,4,256]{3,2,1,0:T(4,128)S(1)} %bitcast.50), channel_id=1, replica_groups=mesh['chip'=16,'core'=2,'ffn'=4,'grp'=4] {'grp'}, dimensions={0} | all-to-all | bytes 65536 | tf_op jit(solution)/shard_map/all_to_all | solution.py:16
  49.5 0.2 exponential_reduce_fusion
  49.9 11.5 %all_to_all.48 = bf16[32,2,512]{2,1,0:T(2,128)(2,1)S(1)} all-to-all(bf16[32,2,512]{2,1,0:T(2,128)(2,1)S(1)} %broadcast_in_dim.97), channel_id=1, replica_groups=mesh['chip'=16,'core'=2,'ffn'=4,'grp'=4] {'chip','core'}, dimensions={0} | all-to-all | bytes 131072 | tf_op jit(solution)/shard_map/all_to_all | solution.py:16
  61.5 0.3 fusion.2
  61.8 0.7 broadcast_in_dim.154
  62.4 3.3 %all-to-all-start.5 = ((bf16[4,64,256]{2,1,0:T(8,128)(2,1)}), bf16[4,64,256]{2,1,0:T(8,128)(2,1)S(1)}, u32[]{:S(2)}, u32[]{:S(2)}) async-start(bf16[4,64,256]{2,1,0:T(8,128)(2,1)} %broadcast_in_dim.154), calls=%async_computation.5 | async-start | bytes 262144 | tf_op jit(solution)/shard_map/all_to_all | solution.py:16
  65.8 5.9 %all-to-all-done.5 = bf16[4,64,256]{2,1,0:T(8,128)(2,1)S(1)} async-done(((bf16[4,64,256]{2,1,0:T(8,128)(2,1)}), bf16[4,64,256]{2,1,0:T(8,128)(2,1)S(1)}, u32[]{:S(2)}, u32[]{:S(2)}) %all-to-all-start.5) | async-done | bytes 131104 | tf_op jit(solution)/shard_map/all_to_all | solution.py:16
  71.7 11.8 %conditional.4 = (f32[64,256]{1,0:T(8,128)S(1)}) conditional(s32[]{:T(128)} %convert_element_type.211, () %tuple.41, bf16[64,256]{1,0:T(8,128)(2,1)S(1)} %reduce_sum.124), branch_computations={%region_11.12_spmd, %region_12.13_spmd} | conditional | flops 16384 | bytes 229424 | solution.py:54
  71.8 9.1 %collective-permute-start = (bf16[64,256]{1,0:T(8,128)(2,1)S(1)}, bf16[64,256]{1,0:T(8,128)(2,1)S(1)}, u32[]{:S(2)}, u32[]{:S(2)}) collective-permute-start(bf16[64,256]{1,0:T(8,128)(2,1)S(1)} %param.1), channel_id=1, source_target_pairs={{0,4},{4,0},{1,5},{5,1},{2,6},{6,2},{3,7},{7,3},{16,20},{20,16},{1... | collective-permute-start | bytes 98312 | tf_op jit(solution)/shard_map/cond/branch_1_fun/ppermute | solution.py:44
  80.9 2.7 %collective-permute-done = bf16[64,256]{1,0:T(8,128)(2,1)S(1)} collective-permute-done((bf16[64,256]{1,0:T(8,128)(2,1)S(1)}, bf16[64,256]{1,0:T(8,128)(2,1)S(1)}, u32[]{:S(2)}, u32[]{:S(2)}) %collective-permute-start) | collective-permute-done | bytes 32800 | tf_op jit(solution)/shard_map/cond/branch_1_fun/ppermute | solution.py:44
  83.6 1.3 collective-permute-start.4
  84.9 1.9 %collective-permute-done.4 = bf16[80,256]{1,0:T(8,128)(2,1)S(1)} collective-permute-done((bf16[80,256]{1,0:T(8,128)(2,1)S(1)}, bf16[80,256]{1,0:T(8,128)(2,1)S(1)}, u32[]{:S(2)}, u32[]{:S(2)}) %collective-permute-start.4) | collective-permute-done | bytes 40992 | tf_op jit(solution)/shard_map/ppermute | solution.py:47
  86.8 1.3 collective-permute-start.5
  88.2 1.6 %copy.40 = bf16[32,8,2,1664]{3,1,2,0:T(8,128)(2,1)S(1)} copy(bf16[32,8,2,1664]{3,2,1,0:T(2,128)(2,1)} %bitcast.49) | data formatting | bytes 3407872
  89.8 6.7 %collective-permute-done.5 = bf16[64,256]{1,0:T(8,128)(2,1)S(1)} collective-permute-done((bf16[64,256]{1,0:T(8,128)(2,1)S(1)}, bf16[64,256]{1,0:T(8,128)(2,1)S(1)}, u32[]{:S(2)}, u32[]{:S(2)}) %collective-permute-start.5) | collective-permute-done | bytes 32800 | tf_op jit(solution)/shard_map/ppermute | solution.py:47
  96.7 0.4 convolution_convert_fusion
  97.2 0.2 reshape.310
  97.4 0.2 dynamic-slice_bitcast_fusion
  97.6 1.9 %collective-permute-start.6 = (bf16[16,2,3456]{2,1,0:T(2,128)(2,1)S(1)}, bf16[16,2,3456]{2,1,0:T(2,128)(2,1)S(1)}, u32[]{:S(2)}, u32[]{:S(2)}) collective-permute-start(bf16[16,2,3456]{2,1,0:T(2,128)(2,1)S(1)} %dynamic-slice_bitcast_fusion), channel_id=1, source_target_pairs={{0,16},{16,0},{1,17},{17,1},{2,18},{18,2},{3,19},{19,3},{4,20},{20... | collective-permute-start | bytes 663560 | tf_op jit(solution)/shard_map/ppermute | solution.py:179
  99.5 1.4 collective-permute-done.6
  101.0 0.2 fusion.3
  101.2 12.1 %all_to_all.49 = bf16[16,2,3456]{2,1,0:T(2,128)(2,1)S(1)} all-to-all(bf16[16,2,3456]{2,1,0:T(2,128)(2,1)S(1)} %fusion.3), channel_id=1, replica_groups=mesh['chip'=16,'core'=2,'ffn'=4,'grp'=4] {'chip'}, dimensions={0} | all-to-all | bytes 442368 | tf_op jit(solution)/shard_map/all_to_all | solution.py:16
  113.3 0.2 convert_reduce_fusion
  113.5 0.2 fusion.31
  113.9 14.1 %all_to_all.50 = bf16[32,2,1664]{2,1,0:T(2,128)(2,1)S(1)} all-to-all(bf16[32,2,1664]{2,1,0:T(2,128)(2,1)S(1)} %broadcast_in_dim.160), channel_id=1, replica_groups=mesh['chip'=16,'core'=2,'ffn'=4,'grp'=4] {'chip','core'}, dimensions={0} | all-to-all | bytes 425984 | tf_op jit(solution)/shard_map/all_to_all | solution.py:16
  128.1 0.3 convolution_convert_fusion.2
  128.4 0.6 broadcast_in_dim.161
  129.0 3.3 %all-to-all-start.8 = ((bf16[4,64,256]{2,1,0:T(8,128)(2,1)}), bf16[4,64,256]{2,1,0:T(8,128)(2,1)S(1)}, u32[]{:S(2)}, u32[]{:S(2)}) async-start(bf16[4,64,256]{2,1,0:T(8,128)(2,1)} %broadcast_in_dim.161), calls=%async_computation.8 | async-start | bytes 262144 | tf_op jit(solution)/shard_map/all_to_all | solution.py:16
  132.4 6.3 %all-to-all-done.8 = bf16[4,64,256]{2,1,0:T(8,128)(2,1)S(1)} async-done(((bf16[4,64,256]{2,1,0:T(8,128)(2,1)}), bf16[4,64,256]{2,1,0:T(8,128)(2,1)S(1)}, u32[]{:S(2)}, u32[]{:S(2)}) %all-to-all-start.8) | async-done | bytes 131104 | tf_op jit(solution)/shard_map/all_to_all | solution.py:16
  138.8 1.3 collective-permute-start.8
  140.1 10.9 %conditional.7 = (f32[64,256]{1,0:T(8,128)S(1)}) conditional(s32[]{:T(128)} %convert_element_type.232, bf16[64,256]{1,0:T(8,128)(2,1)S(1)} %get-tuple-element.48, () %tuple.44), branch_computations={%region_20.21_spmd, %region_21.22_spmd} | conditional | flops 16384 | bytes 229424 | solution.py:58
  140.1 7.7 %collective-permute-start.3 = (bf16[64,256]{1,0:T(8,128)(2,1)S(1)}, bf16[64,256]{1,0:T(8,128)(2,1)S(1)}, u32[]{:S(2)}, u32[]{:S(2)}) collective-permute-start(bf16[64,256]{1,0:T(8,128)(2,1)S(1)} %param.6), channel_id=1, source_target_pairs={{0,4},{4,0},{1,5},{5,1},{2,6},{6,2},{3,7},{7,3},{16,20},{20,16},{1... | collective-permute-start | bytes 98312 | tf_op jit(solution)/shard_map/cond/branch_0_fun/ppermute | solution.py:44
  147.8 3.1 %collective-permute-done.3 = bf16[64,256]{1,0:T(8,128)(2,1)S(1)} collective-permute-done((bf16[64,256]{1,0:T(8,128)(2,1)S(1)}, bf16[64,256]{1,0:T(8,128)(2,1)S(1)}, u32[]{:S(2)}, u32[]{:S(2)}) %collective-permute-start.3) | collective-permute-done | bytes 32800 | tf_op jit(solution)/shard_map/cond/branch_0_fun/ppermute | solution.py:44
  151.0 1.3 collective-permute-start.7
  152.3 1.8 %collective-permute-done.7 = bf16[64,256]{1,0:T(8,128)(2,1)S(1)} collective-permute-done((bf16[64,256]{1,0:T(8,128)(2,1)S(1)}, bf16[64,256]{1,0:T(8,128)(2,1)S(1)}, u32[]{:S(2)}, u32[]{:S(2)}) %collective-permute-start.7) | collective-permute-done | bytes 32800 | tf_op jit(solution)/shard_map/ppermute | solution.py:47
  154.1 0.6 fusion.8
  (77 shorter events, 2.4 us)
Async XLA Ops:
  0.0 128.1 %copy-start = (bf16[1664,256]{1,0:T(8,128)(2,1)S(1)}, bf16[1664,256]{1,0:T(8,128)(2,1)}, u32[]{:S(2)}) copy-start(bf16[1664,256]{1,0:T(8,128)(2,1)} %param.26) | copy-start | bytes 2555908
  0.0 13.6 %copy-start.3 = (bf16[256,1,256]{2,0,1:T(8,128)(2,1)S(1)}, bf16[256,1,256]{2,0,1:T(8,128)(2,1)}, u32[]{:S(2)}) copy-start(bf16[256,1,256]{2,0,1:T(8,128)(2,1)} %param.23) | copy-start | bytes 393220
  0.0 13.6 %copy-start.1 = (bf16[256,512]{1,0:T(8,128)(2,1)S(1)}, bf16[256,512]{1,0:T(8,128)(2,1)}, u32[]{:S(2)}) copy-start(bf16[256,512]{1,0:T(8,128)(2,1)} %param.22) | copy-start | bytes 786436
  0.0 17.8 %copy-start.6 = (f32[256]{0:T(256)S(1)}, f32[256]{0:T(256)}, u32[]{:S(2)}) copy-start(f32[256]{0:T(256)} %param.20) | copy-start | bytes 3076
  1.8 16.0 %all-to-all-start = ((f32[32,1,64]{2,1,0:T(1,128)}), f32[32,1,64]{2,1,0:T(1,128)S(1)}, u32[]{:S(2)}, u32[]{:S(2)}) async-start(f32[32,1,64]{2,1,0:T(1,128)} %broadcast_in_dim.82), calls=%async_computation | async-start | bytes 32768 | tf_op jit(solution)/shard_map/all_to_all | solution.py:16
  18.0 43.4 %copy-start.2 = (bf16[512,256]{1,0:T(8,128)(2,1)S(1)}, bf16[512,256]{1,0:T(8,128)(2,1)}, u32[]{:S(2)}) copy-start(bf16[512,256]{1,0:T(8,128)(2,1)} %param.24) | copy-start | bytes 786436
  18.0 43.4 %copy-start.5 = (s32[64]{0:T(128)S(1)}, s32[64]{0:T(128)}, u32[]{:S(2)}) copy-start(s32[64]{0:T(128)} %param.29) | copy-start | bytes 772
  62.4 9.3 %all-to-all-start.5 = ((bf16[4,64,256]{2,1,0:T(8,128)(2,1)}), bf16[4,64,256]{2,1,0:T(8,128)(2,1)S(1)}, u32[]{:S(2)}, u32[]{:S(2)}) async-start(bf16[4,64,256]{2,1,0:T(8,128)(2,1)} %broadcast_in_dim.154), calls=%async_computation.5 | async-start | bytes 262144 | tf_op jit(solution)/shard_map/all_to_all | solution.py:16
  71.8 11.8 %collective-permute-start = (bf16[64,256]{1,0:T(8,128)(2,1)S(1)}, bf16[64,256]{1,0:T(8,128)(2,1)S(1)}, u32[]{:S(2)}, u32[]{:S(2)}) collective-permute-start(bf16[64,256]{1,0:T(8,128)(2,1)S(1)} %param.1), channel_id=1, source_target_pairs={{0,4},{4,0},{1,5},{5,1},{2,6},{6,2},{3,7},{7,3},{16,20},{20,16},{1... | collective-permute-start | bytes 98312 | tf_op jit(solution)/shard_map/cond/branch_1_fun/ppermute | solution.py:44
  83.6 3.2 %collective-permute-start.4 = (bf16[80,256]{1,0:T(8,128)(2,1)S(1)}, bf16[80,256]{1,0:T(8,128)(2,1)S(1)}, u32[]{:S(2)}, u32[]{:S(2)}) collective-permute-start(bf16[80,256]{1,0:T(8,128)(2,1)S(1)} %pad.7), channel_id=1, source_target_pairs={{0,12},{4,8},{1,13},{5,9},{2,14},{6,10},{3,15},{7,11},{16,28},{20,... | collective-permute-start | bytes 122888 | tf_op jit(solution)/shard_map/ppermute | solution.py:47
  86.8 9.7 %collective-permute-start.5 = (bf16[64,256]{1,0:T(8,128)(2,1)S(1)}, bf16[64,256]{1,0:T(8,128)(2,1)S(1)}, u32[]{:S(2)}, u32[]{:S(2)}) collective-permute-start(bf16[64,256]{1,0:T(8,128)(2,1)S(1)} %broadcast_select_fusion.1), channel_id=1, source_target_pairs={{12,0},{8,4},{13,1},{9,5},{14,2},{10,6},{15,3},{11,7},{28,16},{24,... | collective-permute-start | bytes 98312 | tf_op jit(solution)/shard_map/ppermute | solution.py:47
  88.1 8.4 %copy-start.4 = (bf16[64,256]{1,0:T(8,128)(2,1)S(1)}, bf16[64,256]{1,0:T(8,128)(2,1)}, u32[]{:S(2)}) copy-start(bf16[64,256]{1,0:T(8,128)(2,1)} %param.19) | copy-start | bytes 98308
  88.2 8.5 %copy-start.7 = (f32[256]{0:T(256)S(1)}, f32[256]{0:T(256)}, u32[]{:S(2)}) copy-start(f32[256]{0:T(256)} %param.21) | copy-start | bytes 3076
  97.6 3.4 %collective-permute-start.6 = (bf16[16,2,3456]{2,1,0:T(2,128)(2,1)S(1)}, bf16[16,2,3456]{2,1,0:T(2,128)(2,1)S(1)}, u32[]{:S(2)}, u32[]{:S(2)}) collective-permute-start(bf16[16,2,3456]{2,1,0:T(2,128)(2,1)S(1)} %dynamic-slice_bitcast_fusion), channel_id=1, source_target_pairs={{0,16},{16,0},{1,17},{17,1},{2,18},{18,2},{3,19},{19,3},{4,20},{20... | collective-permute-start | bytes 663560 | tf_op jit(solution)/shard_map/ppermute | solution.py:179
  129.0 9.6 %all-to-all-start.8 = ((bf16[4,64,256]{2,1,0:T(8,128)(2,1)}), bf16[4,64,256]{2,1,0:T(8,128)(2,1)S(1)}, u32[]{:S(2)}, u32[]{:S(2)}) async-start(bf16[4,64,256]{2,1,0:T(8,128)(2,1)} %broadcast_in_dim.161), calls=%async_computation.8 | async-start | bytes 262144 | tf_op jit(solution)/shard_map/all_to_all | solution.py:16
  138.8 15.3 %collective-permute-start.8 = (bf16[80,256]{1,0:T(8,128)(2,1)S(1)}, bf16[80,256]{1,0:T(8,128)(2,1)S(1)}, u32[]{:S(2)}, u32[]{:S(2)}) collective-permute-start(bf16[80,256]{1,0:T(8,128)(2,1)S(1)} %pad.8), channel_id=1, source_target_pairs={{12,0},{8,4},{13,1},{9,5},{14,2},{10,6},{15,3},{11,7},{28,16},{24,... | collective-permute-start | bytes 122888 | tf_op jit(solution)/shard_map/ppermute | solution.py:47
  140.1 10.9 %collective-permute-start.3 = (bf16[64,256]{1,0:T(8,128)(2,1)S(1)}, bf16[64,256]{1,0:T(8,128)(2,1)S(1)}, u32[]{:S(2)}, u32[]{:S(2)}) collective-permute-start(bf16[64,256]{1,0:T(8,128)(2,1)S(1)} %param.6), channel_id=1, source_target_pairs={{0,4},{4,0},{1,5},{5,1},{2,6},{6,2},{3,7},{7,3},{16,20},{20,16},{1... | collective-permute-start | bytes 98312 | tf_op jit(solution)/shard_map/cond/branch_0_fun/ppermute | solution.py:44
  151.0 3.1 %collective-permute-start.7 = (bf16[64,256]{1,0:T(8,128)(2,1)S(1)}, bf16[64,256]{1,0:T(8,128)(2,1)S(1)}, u32[]{:S(2)}, u32[]{:S(2)}) collective-permute-start(bf16[64,256]{1,0:T(8,128)(2,1)S(1)} %add_convert_fusion), channel_id=1, source_target_pairs={{0,12},{4,8},{1,13},{5,9},{2,14},{6,10},{3,15},{7,11},{16,28},{20,... | collective-permute-start | bytes 98312 | tf_op jit(solution)/shard_map/ppermute | solution.py:47

commit v7 on v6

--- a/solution.py
+++ b/solution.py
@@ -50,12 +50,19 @@
         return (one.astype(F32) + two.astype(F32)).astype(BF16)
 
     mine = part.astype(BF16)
-    here = (lax.axis_index(axis) == ahead[0]) | (lax.axis_index(axis) == ahead[1])
-    from_ahead = lax.cond(here, lambda values: swap(values, ahead), jnp.zeros_like, mine)
+    mine, place = lax.optimization_barrier((mine, lax.axis_index(axis)))
+    here = (place == ahead[0]) | (place == ahead[1])
+    if tied:
+        from_ahead = swap(mine, ahead)
+    else:
+        from_ahead = lax.cond(here, lambda values: swap(values, ahead), jnp.zeros_like, mine)
     sum_ahead = add(mine, from_ahead)
     down = hand(jnp.pad(sum_ahead, ((0, 16), (0, 0))), ahead, behind)[: part.shape[0]]
     mine = jnp.where(here, sum_ahead, mine)
-    from_behind = lax.cond(here, jnp.zeros_like, lambda values: swap(values, behind), mine)
+    if tied:
+        from_behind = swap(mine, behind)
+    else:
+        from_behind = lax.cond(here, jnp.zeros_like, lambda values: swap(values, behind), mine)
     sum_behind = add(mine, from_behind)
     sent = jnp.where(here, down, sum_behind) if tied else sum_behind
     up = hand(sent, behind, ahead)

time: 156 us -> 156 us (level)
    ppermute x2 -> x3, starting transfers between devices: 16.8 us -> 17.5 us  [swap(): return lax.ppermute(values, axis, (pair, pair[::-1]))]
    ppermute x2 -> x3, waiting for transfers between devices: 5.86 us -> 5.85 us  [swap(): return lax.ppermute(values, axis, (pair, pair[::-1]))]
  transfers between devices with their start and end apart: 10 -> 11, of which waited for: 9 -> 9; matrix products, arithmetic and copies ran while one was open for 3% -> 3% of each run, Pallas kernels for 0% -> 0%
where the time goes in v7:
time: 156 us; the launch traced here: 155 us
  blocking collectives  67.3 us (43%)
  starting transfers between devices  40.6 us (26%)
  waiting for transfers between devices  33.4 us (21%)
  local copies, waits for them, and re-layouts  5.85 us (4%)
  other arithmetic  4.08 us (3%)
  matrix products  2.92 us (2%)
    all_to_all x6, blocking collectives, exchange(): return lax.all_to_all(parts, axis, 0, 0)  67.3 us
    ppermute x3, starting transfers between devices, swap(): return lax.ppermute(values, axis, (pair, pair[::-1]))  17.5 us
    all_to_all x3, waiting for transfers between devices, exchange(): return lax.all_to_all(parts, axis, 0, 0)  16.4 us
    all_to_all x3, starting transfers between devices, exchange(): return lax.all_to_all(parts, axis, 0, 0)  16.1 us
    ppermute x4, waiting for transfers between devices, hand(): return lax.ppermute(values, axis, tuple(zip(sources, targets)))  9.76 us
    ppermute x3, waiting for transfers between devices, swap(): return lax.ppermute(values, axis, (pair, pair[::-1]))  5.85 us
    ppermute x4, starting transfers between devices, hand(): return lax.ppermute(values, axis, tuple(zip(sources, targets)))  5.17 us
  transfers between devices with their start and end apart: 11, of which 9 were waited for; matrix products, arithmetic and copies ran while one was open for 3% of the time, Pallas kernels for 0%

profile of v7, /device:TPU:2, one launch (start us, length us, event | category | flops | bytes accessed | tf_op | source)
XLA Modules:
  0.0 154.7 jit_solution(1121073095033800826)
XLA Ops:
  0.0 1.1 multiply_reduce_fusion
  1.1 0.6 broadcast_in_dim.82
  1.8 9.4 %all-to-all-start = ((f32[32,1,64]{2,1,0:T(1,128)}), f32[32,1,64]{2,1,0:T(1,128)S(1)}, u32[]{:S(2)}, u32[]{:S(2)}) async-start(f32[32,1,64]{2,1,0:T(1,128)} %broadcast_in_dim.82), calls=%async_computation | async-start | bytes 32768 | tf_op jit(solution)/shard_map/all_to_all | solution.py:16
  11.2 0.8 select_reduce_fusion
  12.0 1.3 slice_bitcast_fusion
  13.6 4.1 %all-to-all-done = f32[32,1,64]{2,1,0:T(1,128)S(1)} async-done(((f32[32,1,64]{2,1,0:T(1,128)}), f32[32,1,64]{2,1,0:T(1,128)S(1)}, u32[]{:S(2)}, u32[]{:S(2)}) %all-to-all-start) | async-done | bytes 8224 | tf_op jit(solution)/shard_map/all_to_all | solution.py:16
  17.8 0.2 fusion.14
  18.1 12.7 %all_to_all.45 = f32[32,2,768]{2,1,0:T(2,128)S(1)} all-to-all(f32[32,2,768]{2,1,0:T(2,128)S(1)} %reshape.303), channel_id=1, replica_groups=mesh['chip'=16,'core'=2,'ffn'=4,'grp'=4] {'chip','core'}, dimensions={0} | all-to-all | bytes 393216 | tf_op jit(solution)/shard_map/all_to_all | solution.py:16
  31.4 9.1 %all_to_all.46 = bf16[4,2,512]{2,1,0:T(2,128)(2,1)S(1)} all-to-all(bf16[4,2,512]{2,1,0:T(2,128)(2,1)S(1)} %broadcast_in_dim.92), channel_id=1, replica_groups=mesh['chip'=16,'core'=2,'ffn'=4,'grp'=4] {'grp'}, dimensions={0} | all-to-all | bytes 16384 | tf_op jit(solution)/shard_map/all_to_all | solution.py:16
  40.5 0.3 fusion.41
  40.9 0.2 fusion.4
  41.0 0.3 fusion.9
  41.6 7.8 %all_to_all.47 = f32[4,2,4,256]{3,2,1,0:T(4,128)S(1)} all-to-all(f32[4,2,4,256]{3,2,1,0:T(4,128)S(1)} %bitcast.50), channel_id=1, replica_groups=mesh['chip'=16,'core'=2,'ffn'=4,'grp'=4] {'grp'}, dimensions={0} | all-to-all | bytes 65536 | tf_op jit(solution)/shard_map/all_to_all | solution.py:16
  49.5 0.2 exponential_reduce_fusion
  49.9 11.5 %all_to_all.48 = bf16[32,2,512]{2,1,0:T(2,128)(2,1)S(1)} all-to-all(bf16[32,2,512]{2,1,0:T(2,128)(2,1)S(1)} %broadcast_in_dim.97), channel_id=1, replica_groups=mesh['chip'=16,'core'=2,'ffn'=4,'grp'=4] {'chip','core'}, dimensions={0} | all-to-all | bytes 131072 | tf_op jit(solution)/shard_map/all_to_all | solution.py:16
  61.5 0.3 fusion.2
  61.8 0.7 broadcast_in_dim.154
  62.4 3.3 %all-to-all-start.5 = ((bf16[4,64,256]{2,1,0:T(8,128)(2,1)}), bf16[4,64,256]{2,1,0:T(8,128)(2,1)S(1)}, u32[]{:S(2)}, u32[]{:S(2)}) async-start(bf16[4,64,256]{2,1,0:T(8,128)(2,1)} %broadcast_in_dim.154), calls=%async_computation.5 | async-start | bytes 262144 | tf_op jit(solution)/shard_map/all_to_all | solution.py:16
  65.8 5.9 %all-to-all-done.5 = bf16[4,64,256]{2,1,0:T(8,128)(2,1)S(1)} async-done(((bf16[4,64,256]{2,1,0:T(8,128)(2,1)}), bf16[4,64,256]{2,1,0:T(8,128)(2,1)S(1)}, u32[]{:S(2)}, u32[]{:S(2)}) %all-to-all-start.5) | async-done | bytes 131104 | tf_op jit(solution)/shard_map/all_to_all | solution.py:16
  71.7 9.1 %collective-permute-start.2 = (bf16[64,256]{1,0:T(8,128)(2,1)S(1)}, bf16[64,256]{1,0:T(8,128)(2,1)S(1)}, u32[]{:S(2)}, u32[]{:S(2)}) collective-permute-start(bf16[64,256]{1,0:T(8,128)(2,1)S(1)} %reduce_sum.122), channel_id=1, source_target_pairs={{0,4},{4,0},{1,5},{5,1},{2,6},{6,2},{3,7},{7,3},{16,20},{20,16},{1... | collective-permute-start | bytes 98312 | tf_op jit(solution)/shard_map/ppermute | solution.py:44
  80.8 2.7 %collective-permute-done.2 = bf16[64,256]{1,0:T(8,128)(2,1)S(1)} collective-permute-done((bf16[64,256]{1,0:T(8,128)(2,1)S(1)}, bf16[64,256]{1,0:T(8,128)(2,1)S(1)}, u32[]{:S(2)}, u32[]{:S(2)}) %collective-permute-start.2) | collective-permute-done | bytes 32800 | tf_op jit(solution)/shard_map/ppermute | solution.py:44
  83.6 1.3 collective-permute-start.4
  84.9 0.7 collective-permute-start.3
  85.6 1.2 collective-permute-done.4
  86.8 1.3 collective-permute-start.5
  88.1 1.6 %copy.40 = bf16[32,8,2,1664]{3,1,2,0:T(8,128)(2,1)S(1)} copy(bf16[32,8,2,1664]{3,2,1,0:T(2,128)(2,1)} %bitcast.49) | data formatting | bytes 3407872
  89.8 6.7 %collective-permute-done.5 = bf16[64,256]{1,0:T(8,128)(2,1)S(1)} collective-permute-done((bf16[64,256]{1,0:T(8,128)(2,1)S(1)}, bf16[64,256]{1,0:T(8,128)(2,1)S(1)}, u32[]{:S(2)}, u32[]{:S(2)}) %collective-permute-start.5) | collective-permute-done | bytes 32800 | tf_op jit(solution)/shard_map/ppermute | solution.py:47
  96.7 0.4 convolution_convert_fusion
  97.2 0.2 reshape.310
  97.4 0.2 dynamic-slice_bitcast_fusion
  97.6 1.9 %collective-permute-start.6 = (bf16[16,2,3456]{2,1,0:T(2,128)(2,1)S(1)}, bf16[16,2,3456]{2,1,0:T(2,128)(2,1)S(1)}, u32[]{:S(2)}, u32[]{:S(2)}) collective-permute-start(bf16[16,2,3456]{2,1,0:T(2,128)(2,1)S(1)} %dynamic-slice_bitcast_fusion), channel_id=1, source_target_pairs={{0,16},{16,0},{1,17},{17,1},{2,18},{18,2},{3,19},{19,3},{4,20},{20... | collective-permute-start | bytes 663560 | tf_op jit(solution)/shard_map/ppermute | solution.py:186
  99.5 1.4 collective-permute-done.6
  100.9 0.2 fusion.3
  101.2 12.1 %all_to_all.49 = bf16[16,2,3456]{2,1,0:T(2,128)(2,1)S(1)} all-to-all(bf16[16,2,3456]{2,1,0:T(2,128)(2,1)S(1)} %fusion.3), channel_id=1, replica_groups=mesh['chip'=16,'core'=2,'ffn'=4,'grp'=4] {'chip'}, dimensions={0} | all-to-all | bytes 442368 | tf_op jit(solution)/shard_map/all_to_all | solution.py:16
  113.3 0.2 convert_reduce_fusion
  113.5 0.2 fusion.31
  113.9 14.1 %all_to_all.50 = bf16[32,2,1664]{2,1,0:T(2,128)(2,1)S(1)} all-to-all(bf16[32,2,1664]{2,1,0:T(2,128)(2,1)S(1)} %broadcast_in_dim.160), channel_id=1, replica_groups=mesh['chip'=16,'core'=2,'ffn'=4,'grp'=4] {'chip','core'}, dimensions={0} | all-to-all | bytes 425984 | tf_op jit(solution)/shard_map/all_to_all | solution.py:16
  128.1 0.3 convolution_convert_fusion.2
  128.4 0.6 broadcast_in_dim.161
  129.0 3.3 %all-to-all-start.8 = ((bf16[4,64,256]{2,1,0:T(8,128)(2,1)}), bf16[4,64,256]{2,1,0:T(8,128)(2,1)S(1)}, u32[]{:S(2)}, u32[]{:S(2)}) async-start(bf16[4,64,256]{2,1,0:T(8,128)(2,1)} %broadcast_in_dim.161), calls=%async_computation.8 | async-start | bytes 262144 | tf_op jit(solution)/shard_map/all_to_all | solution.py:16
  132.3 6.3 %all-to-all-done.8 = bf16[4,64,256]{2,1,0:T(8,128)(2,1)S(1)} async-done(((bf16[4,64,256]{2,1,0:T(8,128)(2,1)}), bf16[4,64,256]{2,1,0:T(8,128)(2,1)S(1)}, u32[]{:S(2)}, u32[]{:S(2)}) %all-to-all-start.8) | async-done | bytes 131104 | tf_op jit(solution)/shard_map/all_to_all | solution.py:16
  138.8 1.3 collective-permute-start.8
  140.1 10.9 %conditional.3 = (f32[64,256]{1,0:T(8,128)S(1)}) conditional(s32[]{:T(128)} %convert_element_type.219, bf16[64,256]{1,0:T(8,128)(2,1)S(1)} %get-tuple-element.46, () %tuple.30), branch_computations={%region_16.17_spmd, %region_17.18_spmd} | conditional | flops 16384 | bytes 229424 | solution.py:65
  140.1 7.7 %collective-permute-start.1 = (bf16[64,256]{1,0:T(8,128)(2,1)S(1)}, bf16[64,256]{1,0:T(8,128)(2,1)S(1)}, u32[]{:S(2)}, u32[]{:S(2)}) collective-permute-start(bf16[64,256]{1,0:T(8,128)(2,1)S(1)} %param.2), channel_id=1, source_target_pairs={{0,4},{4,0},{1,5},{5,1},{2,6},{6,2},{3,7},{7,3},{16,20},{20,16},{1... | collective-permute-start | bytes 98312 | tf_op jit(solution)/shard_map/cond/branch_0_fun/ppermute | solution.py:44
  147.8 3.1 %collective-permute-done.1 = bf16[64,256]{1,0:T(8,128)(2,1)S(1)} collective-permute-done((bf16[64,256]{1,0:T(8,128)(2,1)S(1)}, bf16[64,256]{1,0:T(8,128)(2,1)S(1)}, u32[]{:S(2)}, u32[]{:S(2)}) %collective-permute-start.1) | collective-permute-done | bytes 32800 | tf_op jit(solution)/shard_map/cond/branch_0_fun/ppermute | solution.py:44
  151.0 1.3 collective-permute-start.7
  152.3 1.8 %collective-permute-done.7 = bf16[64,256]{1,0:T(8,128)(2,1)S(1)} collective-permute-done((bf16[64,256]{1,0:T(8,128)(2,1)S(1)}, bf16[64,256]{1,0:T(8,128)(2,1)S(1)}, u32[]{:S(2)}, u32[]{:S(2)}) %collective-permute-start.7) | collective-permute-done | bytes 32800 | tf_op jit(solution)/shard_map/ppermute | solution.py:47
  154.1 0.6 fusion.8
  (75 shorter events, 2.4 us)
Async XLA Ops:
  0.0 128.1 %copy-start = (bf16[1664,256]{1,0:T(8,128)(2,1)S(1)}, bf16[1664,256]{1,0:T(8,128)(2,1)}, u32[]{:S(2)}) copy-start(bf16[1664,256]{1,0:T(8,128)(2,1)} %param.22) | copy-start | bytes 2555908
  0.0 13.6 %copy-start.4 = (bf16[256,1,256]{2,0,1:T(8,128)(2,1)S(1)}, bf16[256,1,256]{2,0,1:T(8,128)(2,1)}, u32[]{:S(2)}) copy-start(bf16[256,1,256]{2,0,1:T(8,128)(2,1)} %param.19) | copy-start | bytes 393220
  0.0 13.6 %copy-start.1 = (bf16[256,512]{1,0:T(8,128)(2,1)S(1)}, bf16[256,512]{1,0:T(8,128)(2,1)}, u32[]{:S(2)}) copy-start(bf16[256,512]{1,0:T(8,128)(2,1)} %param.18) | copy-start | bytes 786436
  0.0 17.8 %copy-start.6 = (f32[256]{0:T(256)S(1)}, f32[256]{0:T(256)}, u32[]{:S(2)}) copy-start(f32[256]{0:T(256)} %param.16) | copy-start | bytes 3076
  1.8 16.0 %all-to-all-start = ((f32[32,1,64]{2,1,0:T(1,128)}), f32[32,1,64]{2,1,0:T(1,128)S(1)}, u32[]{:S(2)}, u32[]{:S(2)}) async-start(f32[32,1,64]{2,1,0:T(1,128)} %broadcast_in_dim.82), calls=%async_computation | async-start | bytes 32768 | tf_op jit(solution)/shard_map/all_to_all | solution.py:16
  18.0 43.4 %copy-start.2 = (bf16[512,256]{1,0:T(8,128)(2,1)S(1)}, bf16[512,256]{1,0:T(8,128)(2,1)}, u32[]{:S(2)}) copy-start(bf16[512,256]{1,0:T(8,128)(2,1)} %param.20) | copy-start | bytes 786436
  18.0 43.4 %copy-start.5 = (s32[64]{0:T(128)S(1)}, s32[64]{0:T(128)}, u32[]{:S(2)}) copy-start(s32[64]{0:T(128)} %param.25) | copy-start | bytes 772
  62.4 9.3 %all-to-all-start.5 = ((bf16[4,64,256]{2,1,0:T(8,128)(2,1)}), bf16[4,64,256]{2,1,0:T(8,128)(2,1)S(1)}, u32[]{:S(2)}, u32[]{:S(2)}) async-start(bf16[4,64,256]{2,1,0:T(8,128)(2,1)} %broadcast_in_dim.154), calls=%async_computation.5 | async-start | bytes 262144 | tf_op jit(solution)/shard_map/all_to_all | solution.py:16
  71.7 11.8 %collective-permute-start.2 = (bf16[64,256]{1,0:T(8,128)(2,1)S(1)}, bf16[64,256]{1,0:T(8,128)(2,1)S(1)}, u32[]{:S(2)}, u32[]{:S(2)}) collective-permute-start(bf16[64,256]{1,0:T(8,128)(2,1)S(1)} %reduce_sum.122), channel_id=1, source_target_pairs={{0,4},{4,0},{1,5},{5,1},{2,6},{6,2},{3,7},{7,3},{16,20},{20,16},{1... | collective-permute-start | bytes 98312 | tf_op jit(solution)/shard_map/ppermute | solution.py:44
  83.6 3.2 %collective-permute-start.4 = (bf16[80,256]{1,0:T(8,128)(2,1)S(1)}, bf16[80,256]{1,0:T(8,128)(2,1)S(1)}, u32[]{:S(2)}, u32[]{:S(2)}) collective-permute-start(bf16[80,256]{1,0:T(8,128)(2,1)S(1)} %pad.7), channel_id=1, source_target_pairs={{0,12},{4,8},{1,13},{5,9},{2,14},{6,10},{3,15},{7,11},{16,28},{20,... | collective-permute-start | bytes 122888 | tf_op jit(solution)/shard_map/ppermute | solution.py:47
  84.9 0.7 collective-permute-start.3
  86.8 9.7 %collective-permute-start.5 = (bf16[64,256]{1,0:T(8,128)(2,1)S(1)}, bf16[64,256]{1,0:T(8,128)(2,1)S(1)}, u32[]{:S(2)}, u32[]{:S(2)}) collective-permute-start(bf16[64,256]{1,0:T(8,128)(2,1)S(1)} %broadcast_select_fusion.1), channel_id=1, source_target_pairs={{12,0},{8,4},{13,1},{9,5},{14,2},{10,6},{15,3},{11,7},{28,16},{24,... | collective-permute-start | bytes 98312 | tf_op jit(solution)/shard_map/ppermute | solution.py:47
  88.1 8.4 %copy-start.3 = (bf16[64,256]{1,0:T(8,128)(2,1)S(1)}, bf16[64,256]{1,0:T(8,128)(2,1)}, u32[]{:S(2)}) copy-start(bf16[64,256]{1,0:T(8,128)(2,1)} %param.15) | copy-start | bytes 98308
  88.1 8.5 %copy-start.7 = (f32[256]{0:T(256)S(1)}, f32[256]{0:T(256)}, u32[]{:S(2)}) copy-start(f32[256]{0:T(256)} %param.17) | copy-start | bytes 3076
  97.6 3.4 %collective-permute-start.6 = (bf16[16,2,3456]{2,1,0:T(2,128)(2,1)S(1)}, bf16[16,2,3456]{2,1,0:T(2,128)(2,1)S(1)}, u32[]{:S(2)}, u32[]{:S(2)}) collective-permute-start(bf16[16,2,3456]{2,1,0:T(2,128)(2,1)S(1)} %dynamic-slice_bitcast_fusion), channel_id=1, source_target_pairs={{0,16},{16,0},{1,17},{17,1},{2,18},{18,2},{3,19},{19,3},{4,20},{20... | collective-permute-start | bytes 663560 | tf_op jit(solution)/shard_map/ppermute | solution.py:186
  129.0 9.6 %all-to-all-start.8 = ((bf16[4,64,256]{2,1,0:T(8,128)(2,1)}), bf16[4,64,256]{2,1,0:T(8,128)(2,1)S(1)}, u32[]{:S(2)}, u32[]{:S(2)}) async-start(bf16[4,64,256]{2,1,0:T(8,128)(2,1)} %broadcast_in_dim.161), calls=%async_computation.8 | async-start | bytes 262144 | tf_op jit(solution)/shard_map/all_to_all | solution.py:16
  138.8 15.3 %collective-permute-start.8 = (bf16[80,256]{1,0:T(8,128)(2,1)S(1)}, bf16[80,256]{1,0:T(8,128)(2,1)S(1)}, u32[]{:S(2)}, u32[]{:S(2)}) collective-permute-start(bf16[80,256]{1,0:T(8,128)(2,1)S(1)} %pad.8), channel_id=1, source_target_pairs={{12,0},{8,4},{13,1},{9,5},{14,2},{10,6},{15,3},{11,7},{28,16},{24,... | collective-permute-start | bytes 122888 | tf_op jit(solution)/shard_map/ppermute | solution.py:47
  140.1 10.9 %collective-permute-start.1 = (bf16[64,256]{1,0:T(8,128)(2,1)S(1)}, bf16[64,256]{1,0:T(8,128)(2,1)S(1)}, u32[]{:S(2)}, u32[]{:S(2)}) collective-permute-start(bf16[64,256]{1,0:T(8,128)(2,1)S(1)} %param.2), channel_id=1, source_target_pairs={{0,4},{4,0},{1,5},{5,1},{2,6},{6,2},{3,7},{7,3},{16,20},{20,16},{1... | collective-permute-start | bytes 98312 | tf_op jit(solution)/shard_map/cond/branch_0_fun/ppermute | solution.py:44
  151.0 3.1 %collective-permute-start.7 = (bf16[64,256]{1,0:T(8,128)(2,1)S(1)}, bf16[64,256]{1,0:T(8,128)(2,1)S(1)}, u32[]{:S(2)}, u32[]{:S(2)}) collective-permute-start(bf16[64,256]{1,0:T(8,128)(2,1)S(1)} %add_convert_fusion), channel_id=1, source_target_pairs={{0,12},{4,8},{1,13},{5,9},{2,14},{6,10},{3,15},{7,11},{16,28},{20,... | collective-permute-start | bytes 98312 | tf_op jit(solution)/shard_map/ppermute | solution.py:47
